TPU v7x, 512 devices: a whole 4x8x8 slice. The times are simulated.
512 devices in a mesh: rad: 32 (over z, y_hi), azi: 16 (over y_lo, x, core).
Axes of the slice: x: 4, y: 8 (y_hi: 4, y_lo: 2; y = y_hi * 2 + y_lo), z: 8, core: 2. Of those that a mesh axis runs over, the one named last changes fastest.
Arguments:
- density: float32 [512, 2048, 128], P('rad', 'azi'), may hold values from -6 to 6
Outputs:
- potential: float32 [512, 2048, 128], P('rad', 'azi')
All inputs are finite; a program needn't handle non-finite values.
Results may differ from a plain program's by a relative error of at most 0.000073.
Values sent between devices are 32-bit elements; how exact they have to be, the bound alone decides.
No kernel may reach another device: no remote copies, remote signals or barrier semaphores. Data moves between devices by JAX's collectives and lax.ppermute only.
A program may use at most 64 MiB of HBM per device.

v0:
```python
import math

import jax
import jax.numpy as jnp
from jax import lax
from jax.sharding import PartitionSpec as P

NPHI = 2048
MODES = 256
SWEEPS = 4


low_bound = 0.1
high_bound = 2.0
theta = 0.5 * (high_bound + low_bound)
delta = 0.5 * (high_bound - low_bound)
sigma = theta / delta
four_pi = 4.0 * math.pi


def with_halo(block, sides, width):
    for axis, dim in sides:
        count = lax.axis_size(axis)
        forward = [(i, i + 1) for i in range(count - 1)]
        backward = [(target, source) for source, target in forward]
        low = lax.ppermute(
            lax.slice_in_dim(block, block.shape[dim] - width, None, axis=dim), axis, forward
        )
        high = lax.ppermute(lax.slice_in_dim(block, 0, width, axis=dim), axis, backward)
        block = jnp.concatenate([low, block, high], axis=dim)
    return block


def basis(mode_first, mode_count, phi_first, phi_count, length, forward):
    modes = mode_first + jnp.arange(mode_count, dtype=jnp.int32)
    cells = phi_first + jnp.arange(phi_count, dtype=jnp.int32)
    product = cells[:, None] * modes[None, :] % length
    angle = product.astype(jnp.float32) * (2.0 * math.pi / length)
    if forward:
        weight = jnp.full((mode_count,), 1.0 / length, jnp.float32)
    else:
        weight = jnp.where(modes == 0, 1.0, 2.0).astype(jnp.float32)
    table = jnp.stack([jnp.cos(angle) * weight, jnp.sin(angle) * weight], axis=2)
    return table.reshape(phi_count, 2 * mode_count)


def extend(field):
    return with_halo(field, (("rad", 2),), 1)


def solve(source, mode_first, radius_first, widen):
    count, _, rows, depth = source.shape
    modes = (mode_first + jnp.arange(count, dtype=jnp.int32)).astype(jnp.float32)
    radius = (radius_first + jnp.arange(rows, dtype=jnp.int32)).astype(jnp.float32) + 0.5
    diagonal = (
        4.0 + modes[:, None] * modes[:, None] / (radius[None, :] * radius[None, :])
    ).reshape(count, 1, rows, 1)
    outer_weight = (1.0 + 0.5 / radius).reshape(1, 1, rows, 1)
    inner_weight = (1.0 - 0.5 / radius).reshape(1, 1, rows, 1)
    ratio = 1.0 / sigma
    update = source / diagonal / theta
    iterate = update
    for sweep in range(SWEEPS - 1):
        padded = widen(iterate)
        vertical = jnp.pad(iterate, ((0, 0), (0, 0), (0, 0), (1, 1)))
        image = (
            diagonal * iterate
            - outer_weight * padded[:, :, 2:, :]
            - inner_weight * padded[:, :, :-2, :]
        )
        image = image - vertical[:, :, :, 2:] - vertical[:, :, :, :-2]
        residual = source - image
        next_ratio = 1.0 / (2.0 * sigma - ratio)
        update = next_ratio * ratio * update + 2.0 * next_ratio / delta * (residual / diagonal)
        iterate = iterate + update
        ratio = next_ratio
    return iterate


def per_device(density):
    r_dev, phi_dev, depth = density.shape
    modes_dev = MODES // lax.axis_size("azi")
    sector = lax.axis_index("azi")
    mode_first = sector * modes_dev
    phi_first = sector * phi_dev
    piece = lax.all_gather(density, "azi", axis=1, tiled=True)
    table = basis(mode_first, modes_dev, jnp.int32(0), piece.shape[1], NPHI, True)
    spectrum = jnp.einsum("rjz,jk->krz", piece, table, precision=lax.Precision.HIGHEST)
    spectrum = spectrum.reshape(modes_dev, 2, r_dev, depth)
    radius_first = lax.axis_index("rad") * r_dev
    source = -four_pi * spectrum
    solved = solve(source, mode_first, radius_first, extend)
    piece = lax.all_gather(solved, "azi", axis=0, tiled=True)
    count = piece.shape[0]
    table = basis(jnp.int32(0), count, phi_first, phi_dev, NPHI, False)
    flat = piece.reshape(2 * count, r_dev, depth)
    return jnp.einsum("krz,jk->rjz", flat, table, precision=lax.Precision.HIGHEST)


def solution(mesh):
    in_specs = (P("rad", "azi", None),)
    out_specs = P("rad", "azi", None)
    return jax.shard_map(
        per_device, mesh=mesh, in_specs=in_specs, out_specs=out_specs, check_vma=False
    )
```

profile of v0, /device:TPU:1, one launch (start us, length us, event | category | flops | bytes accessed | tf_op | source)
XLA Modules:
  0.0 217.8 jit_solution(7788796715064218750)
XLA Ops:
  6.5 0.0 all-gather.3.cloned.1.call-start
  6.5 0.7 all-gather.3.cloned.1.call-update
  7.3 0.0 all-gather.5.cloned.1.call-start
  7.3 0.6 cosine_multiply_fusion
  8.0 0.2 copy.5
  8.2 0.2 reshape.322
  8.4 0.1 dot_general.11
  8.5 0.1 broadcast_multiply_fusion
  8.6 103.7 %all-gather.3.cloned.1.call-done = f32[16,2048,128]{2,1,0:T(8,128)} async-done(((f32[16,128,128]{2,1,0:T(8,128)}), f32[16,2048,128]{2,1,0:T(8,128)}) %all-gather.3.cloned.1.call-update) | async-done | bytes 16777232 | tf_op jit(solution)/shard_map/all_gather | solution.py:86
  112.4 13.3 %divide_multiply_fusion = (f32[16,2,16,128]{3,0,2,1:T(8,128)S(1)}, f32[16,2,16,128]{3,0,2,1:T(8,128)S(1)}) fusion(f32[16,16]{0,1:T(8,128)S(1)} %get-tuple-element.18, f32[16,2048,128]{2,1,0:T(8,128)} %all-gather.3.cloned.1.call-done, f32[16,2,2048,1]{2,1,0,3:T(2,128)S(1)} %bitcast.24), kind=kOutput, calls=%fused_computation.53 | convolution fusion | flops 1610809344 | bytes 17564672 | tf_op jit(solution)/shard_map/rjz,jk->krz/dot_general | solution.py:88
  125.6 1.3 collective-permute-start
  126.9 4.9 %collective-permute-start.1 = (f32[16,2,1,128]{3,0,2,1:T(8,128)S(1)}, f32[16,2,1,128]{3,0,2,1:T(8,128)S(1)}, u32[]{:S(2)}, u32[]{:S(2)}) collective-permute-start(f32[16,2,1,128]{3,0,2,1:T(8,128)S(1)} %get-tuple-element.14), channel_id=1, source_target_pairs={{0,16},{16,32},{32,48},{48,64},{64,80},{80,96},{96,112},{112,128},... | collective-permute-start | bytes 49160 | tf_op jit(solution)/shard_map/ppermute | solution.py:26
  131.9 0.0 collective-permute-done
  131.9 0.8 collective-permute-done.1
  132.7 0.3 fusion.58
  133.0 1.3 collective-permute-start.2
  134.3 5.8 %collective-permute-start.3 = (f32[16,2,1,128]{3,0,2,1:T(8,128)S(1)}, f32[16,2,1,128]{3,0,2,1:T(8,128)S(1)}, u32[]{:S(2)}, u32[]{:S(2)}) collective-permute-start(f32[16,2,1,128]{3,0,2,1:T(8,128)S(1)} %get-tuple-element.12), channel_id=1, source_target_pairs={{0,16},{16,32},{32,48},{48,64},{64,80},{80,96},{96,112},{112,128},... | collective-permute-start | bytes 49160 | tf_op jit(solution)/shard_map/ppermute | solution.py:26
  140.2 0.0 collective-permute-done.2
  140.2 0.8 collective-permute-done.3
  141.0 0.3 fusion.56
  141.3 1.3 collective-permute-start.4
  142.6 6.4 %collective-permute-start.5 = (f32[16,2,1,128]{3,0,2,1:T(8,128)S(1)}, f32[16,2,1,128]{3,0,2,1:T(8,128)S(1)}, u32[]{:S(2)}, u32[]{:S(2)}) collective-permute-start(f32[16,2,1,128]{3,0,2,1:T(8,128)S(1)} %get-tuple-element.10), channel_id=1, source_target_pairs={{0,16},{16,32},{32,48},{48,64},{64,80},{80,96},{96,112},{112,128},... | collective-permute-start | bytes 49160 | tf_op jit(solution)/shard_map/ppermute | solution.py:26
  149.0 0.0 collective-permute-done.4
  149.0 0.8 collective-permute-done.5
  149.9 1.0 fusion.23
  150.9 0.0 all-gather.5.cloned.1.call-update
  150.9 0.6 cosine_multiply_fusion.1
  151.5 54.0 %all-gather.5.cloned.1.call-done = f32[256,2,16,128]{3,0,2,1:T(8,128)} async-done(((f32[16,2,16,128]{3,0,2,1:T(8,128)}), f32[256,2,16,128]{3,0,2,1:T(8,128)}) %all-gather.5.cloned.1.call-update) | async-done | bytes 4194320 | tf_op jit(solution)/shard_map/all_gather | solution.py:93
  205.5 5.5 %convolution_bitcast_fusion = f32[16,128,128]{2,1,0:T(8,128)} fusion(f32[256,2,16,128]{3,0,2,1:T(8,128)} %all-gather.5.cloned.1.call-done, f32[128,256,1]{1,0,2:T(8,128)S(1)} %get-tuple-element.16, f32[128,256,1]{1,0,2:T(8,128)S(1)} %get-tuple-element.15), kind=kOutput, calls=%fused_computation.2 | convolution fusion | flops 1610678272 | bytes 5505024 | tf_op jit(solution)/shard_map/krz,jk->rjz/dot_general | solution.py:97
  (9 shorter events, 0.1 us)
Async XLA Ops:
  6.5 105.8 %all-gather.3.cloned.1.call-start = ((), (), s32[]{:S(2)}) async-start(), calls=%async_computation | async-start | bytes 17825792 | tf_op jit(solution)/shard_map/all_gather | solution.py:86
  7.3 198.2 %all-gather.5.cloned.1.call-start = ((), (), s32[]{:S(2)}) async-start(), calls=%async_computation.1 | async-start | bytes 4456448 | tf_op jit(solution)/shard_map/all_gather | solution.py:93
  125.6 6.2 %collective-permute-start = (f32[16,2,1,128]{3,0,2,1:T(8,128)S(1)}, f32[16,2,1,128]{3,0,2,1:T(8,128)S(1)}, u32[]{:S(2)}, u32[]{:S(2)}) collective-permute-start(f32[16,2,1,128]{3,0,2,1:T(8,128)S(1)} %get-tuple-element.13), channel_id=1, source_target_pairs={{16,0},{32,16},{48,32},{64,48},{80,64},{96,80},{112,96},{128,112},... | collective-permute-start | bytes 49160 | tf_op jit(solution)/shard_map/ppermute | solution.py:29
  126.9 5.7 %collective-permute-start.1 = (f32[16,2,1,128]{3,0,2,1:T(8,128)S(1)}, f32[16,2,1,128]{3,0,2,1:T(8,128)S(1)}, u32[]{:S(2)}, u32[]{:S(2)}) collective-permute-start(f32[16,2,1,128]{3,0,2,1:T(8,128)S(1)} %get-tuple-element.14), channel_id=1, source_target_pairs={{0,16},{16,32},{32,48},{48,64},{64,80},{80,96},{96,112},{112,128},... | collective-permute-start | bytes 49160 | tf_op jit(solution)/shard_map/ppermute | solution.py:26
  133.0 7.1 %collective-permute-start.2 = (f32[16,2,1,128]{3,0,2,1:T(8,128)S(1)}, f32[16,2,1,128]{3,0,2,1:T(8,128)S(1)}, u32[]{:S(2)}, u32[]{:S(2)}) collective-permute-start(f32[16,2,1,128]{3,0,2,1:T(8,128)S(1)} %get-tuple-element.11), channel_id=1, source_target_pairs={{16,0},{32,16},{48,32},{64,48},{80,64},{96,80},{112,96},{128,112},... | collective-permute-start | bytes 49160 | tf_op jit(solution)/shard_map/ppermute | solution.py:29
  134.3 6.7 %collective-permute-start.3 = (f32[16,2,1,128]{3,0,2,1:T(8,128)S(1)}, f32[16,2,1,128]{3,0,2,1:T(8,128)S(1)}, u32[]{:S(2)}, u32[]{:S(2)}) collective-permute-start(f32[16,2,1,128]{3,0,2,1:T(8,128)S(1)} %get-tuple-element.12), channel_id=1, source_target_pairs={{0,16},{16,32},{32,48},{48,64},{64,80},{80,96},{96,112},{112,128},... | collective-permute-start | bytes 49160 | tf_op jit(solution)/shard_map/ppermute | solution.py:26
  141.3 7.7 %collective-permute-start.4 = (f32[16,2,1,128]{3,0,2,1:T(8,128)S(1)}, f32[16,2,1,128]{3,0,2,1:T(8,128)S(1)}, u32[]{:S(2)}, u32[]{:S(2)}) collective-permute-start(f32[16,2,1,128]{3,0,2,1:T(8,128)S(1)} %get-tuple-element.9), channel_id=1, source_target_pairs={{16,0},{32,16},{48,32},{64,48},{80,64},{96,80},{112,96},{128,112},... | collective-permute-start | bytes 49160 | tf_op jit(solution)/shard_map/ppermute | solution.py:29
  142.6 7.3 %collective-permute-start.5 = (f32[16,2,1,128]{3,0,2,1:T(8,128)S(1)}, f32[16,2,1,128]{3,0,2,1:T(8,128)S(1)}, u32[]{:S(2)}, u32[]{:S(2)}) collective-permute-start(f32[16,2,1,128]{3,0,2,1:T(8,128)S(1)} %get-tuple-element.10), channel_id=1, source_target_pairs={{0,16},{16,32},{32,48},{48,64},{64,80},{80,96},{96,112},{112,128},... | collective-permute-start | bytes 49160 | tf_op jit(solution)/shard_map/ppermute | solution.py:26
Sparse Core Ops, SparseCore 0:
  9.5 102.8 all-gather.2
  151.0 54.4 all-gather.4
where the time goes:
time: 218 us
  waiting for transfers between devices  161 us (74%)
  starting transfers between devices  21 us (10%)
  matrix products  18.8 us (9%)
  between operations  13.6 us (6%)
  other arithmetic  2.9 us (1%)
    all_gather x1, waiting for transfers between devices, per_device(): piece = lax.all_gather(density, 'azi', axis=1, tiled=True)  104 us
    all_gather x1, waiting for transfers between devices, per_device(): piece = lax.all_gather(solved, 'azi', axis=0, tiled=True)  54 us
    ppermute x3, starting transfers between devices, with_halo(): lax.ppermute(lax.slice_in_dim(block, block.shape[dim] - width, None, axis...  17.1 us
    dot_general x1, matrix products, per_device(): jnp.einsum('rjz,jk->krz', piece, table, precision=lax.Precision.HIGHEST)  13.3 us
    dot_general x1, matrix products, per_device(): jnp.einsum('krz,jk->rjz', flat, table, precision=lax.Precision.HIGHEST)  5.5 us
  transfers between devices with their start and end apart: 8, of which 5 were waited for; matrix products, arithmetic and copies ran while one was open for 1% of the time, Pallas kernels for 0%

commit v1 on v0

v1 whole, which is shorter than its diff:
```python
import functools
import math

import jax
import jax.numpy as jnp
import numpy as np
from jax import lax
from jax.experimental import pallas as pl
from jax.experimental.pallas import tpu as pltpu
from jax.sharding import PartitionSpec as P

NPHI = 2048
MODES = 256
SWEEPS = 4
SECTORS = 16
SECTOR = NPHI // SECTORS
COEFS = 2 * MODES
RANK = 48
ROWS = 16
DEPTH = 128
GROUP = 8
LANES = 128

low_bound = 0.1
high_bound = 2.0
theta = 0.5 * (high_bound + low_bound)
delta = 0.5 * (high_bound - low_bound)
sigma = theta / delta
four_pi = 4.0 * math.pi

BF = jnp.bfloat16
F32 = jnp.float32


def split_table(table):
    high = table.astype(np.float32).astype(BF)
    low = (table - high.astype(np.float64)).astype(np.float32).astype(BF)
    return high, low


@functools.cache
def tables():
    modes = np.arange(MODES)
    angle = 2.0 * np.pi * ((np.arange(SECTOR)[:, None] * modes[None, :]) % NPHI) / NPHI
    first = np.concatenate([np.cos(angle), np.sin(angle)], axis=1)
    left, _, _ = np.linalg.svd(first, full_matrices=False)
    left = left[:, :RANK]
    cores = []
    for sector in range(SECTORS):
        cells = sector * SECTOR + np.arange(SECTOR)
        angle = 2.0 * np.pi * ((cells[:, None] * modes[None, :]) % NPHI) / NPHI
        cores.append(left.T @ np.concatenate([np.cos(angle), np.sin(angle)], axis=1))
    core = np.concatenate(cores, axis=0)
    weight = np.where(np.tile(modes, 2) == 0, 1.0, 2.0)
    left_high, left_low = split_table(left)
    forward = split_table(core.T * (-four_pi / NPHI))
    inverse = split_table(core * weight[None, :])
    squeeze = np.concatenate(
        [
            np.concatenate([left_high.T, left_high.T], axis=1),
            np.concatenate([left_low.T, left_low.T], axis=1),
        ],
        axis=0,
    )
    stretch = np.concatenate([left_high, left_high, left_low, left_low], axis=1)
    return squeeze, forward, inverse, stretch


def halves(value):
    high = value.astype(BF)
    low = (value - high.astype(F32)).astype(BF)
    return high, low


def dot(a, b):
    return jnp.dot(a, b, preferred_element_type=F32)


def lane_group(shape):
    return lax.broadcasted_iota(jnp.int32, shape, 1) // GROUP


def swap_groups(blocks):
    blocks = list(blocks)
    group = lane_group(blocks[0].shape)
    for bit in (1, 2, 4, 8):
        keep = (group & bit) == 0
        for i in range(16):
            if i & bit:
                continue
            j = i | bit
            one, two = blocks[i], blocks[j]
            blocks[i] = jnp.where(keep, one, pltpu.roll(two, GROUP * bit, 1))
            blocks[j] = jnp.where(keep, pltpu.roll(one, LANES - GROUP * bit, 1), two)
    return blocks


def compress_kernel(x_ref, squeeze_ref, out_ref, y_ref):
    squeeze = squeeze_ref[...]
    for r in range(0, ROWS, 2):
        columns = []
        for k in range(2):
            columns.append(jnp.concatenate(halves(x_ref[r + k]), axis=0))
        y = dot(squeeze, jnp.concatenate(columns, axis=1))
        y = y[:RANK] + y[RANK:]
        y_ref[r] = y[:, :LANES]
        y_ref[r + 1] = y[:, LANES:]
    inside = lax.broadcasted_iota(jnp.int32, (8, LANES), 1) % GROUP
    for c in range(0, RANK, 8):
        rows = [pltpu.roll(y_ref[r, c : c + 8, :], 4, 1) for r in range(ROWS)]
        groups = swap_groups(rows)
        edge = groups[0]
        groups[0] = jnp.where(inside >= 4, edge, 0.0)
        groups.append(jnp.where(inside < 4, edge, 0.0))
        for q in range(SECTORS):
            out_ref[q, c : c + 8, :LANES] = groups[q]
            out_ref[q, c : c + 8, LANES:] = groups[q + 1]


def source_kernel(p_ref, high_ref, low_ref, s_ref, down_ref, up_ref):
    p_high, p_low = halves(p_ref[...])
    step = 128
    for m in range(0, COEFS, step):
        w_high = high_ref[m : m + step, :]
        w_low = low_ref[m : m + step, :]
        s_ref[m : m + step, :] = dot(w_high, p_high) + dot(w_high, p_low) + dot(w_low, p_high)
    lane = lax.broadcasted_iota(jnp.int32, (8, LANES), 1)
    for m in range(0, MODES, 8):
        pieces = [
            s_ref[half + m : half + m + 8, h : h + LANES]
            for half in (0, MODES)
            for h in (0, LANES)
        ]
        down = pieces[0]
        up = pltpu.roll(pieces[0], 24, 1)
        for k in (1, 2, 3):
            down = jnp.where(lane < 24 * k, down, pltpu.roll(pieces[k], 24 * k, 1))
            up = jnp.where(lane < 24 * k, up, pltpu.roll(pieces[k], 24 * k + 24, 1))
        down_ref[m : m + 8, :] = down
        up_ref[m : m + 8, :] = up


def solve_kernel(place_ref, s_ref, low_ref, high_ref, vh_ref, vl_ref, out_ref, own_ref):
    shape = (8, LANES)
    lane = lax.broadcasted_iota(jnp.int32, shape, 1)
    slot = lane // GROUP
    inside = lane % GROUP
    row_first = place_ref[0]
    row_count = place_ref[1]
    depth_first = place_ref[2]
    main_row = slot + row_first
    halo_row = jnp.where(slot < 8, slot + 16, slot - 16) + row_first
    depths = [depth_first - 4 + h * GROUP + inside for h in range(2)]
    last, first = slot == 15, slot == 0

    def weights(row):
        radius = row.astype(F32) + 0.5
        inverse = 1.0 / radius
        return 1.0 + 0.5 * inverse, 1.0 - 0.5 * inverse, inverse * inverse

    main_out, main_in, main_square = weights(main_row)
    halo_out, halo_in, halo_square = weights(halo_row)

    def valid(row, depth):
        good = (row >= 0) & (row < row_count) & (depth >= 0) & (depth < DEPTH)
        return jnp.where(good, 1.0, 0.0).astype(F32)

    main_valid = [valid(main_row, d) for d in depths]
    halo_valid = [valid(halo_row, d) for d in depths]

    def turn(value, amount):
        return pltpu.roll(value, amount % LANES, 1)

    def vertical(pair):
        lower, upper = pair
        return [
            jnp.where(inside == 7, turn(upper, 7), turn(lower, -1)) + turn(lower, 1),
            turn(upper, -1) + jnp.where(inside == 0, turn(lower, -7), turn(upper, 1)),
        ]

    ratios = []
    ratio = 1.0 / sigma
    for _ in range(SWEEPS - 1):
        following = 1.0 / (2.0 * sigma - ratio)
        ratios.append((following * ratio, 2.0 * following / delta))
        ratio = following

    @pl.loop(0, MODES // 8, unroll=2)
    def _(group):
        m = pl.multiple_of(group * 8, 8)
        mode = (lax.broadcasted_iota(jnp.int32, shape, 0) + m).astype(F32)
        square = mode * mode
        main_inv = 1.0 / (4.0 + square * main_square)
        halo_inv = 1.0 / (4.0 + square * halo_square)
        main_invs = [main_inv * v for v in main_valid]
        halo_invs = [halo_inv * v for v in halo_valid]
        low = low_ref[pl.ds(m, 8), :]
        high = high_ref[pl.ds(m, 8), :]
        for part in range(2):
            at = pl.multiple_of(part * MODES + m, 8)
            main_s = [s_ref[pl.ds(at, 8), h * LANES : (h + 1) * LANES] for h in range(2)]
            halo_s = []
            for h in range(2):
                k = 2 * part + h
                after = turn(high, -24 * k)
                before = turn(low, 104 - 24 * k)
                halo_s.append(
                    jnp.where(slot < 3, after, jnp.where(slot >= 13, before, 0.0))
                )
            main_u = [s * i * (1.0 / theta) for s, i in zip(main_s, main_invs)]
            halo_u = [s * i * (1.0 / theta) for s, i in zip(halo_s, halo_invs)]
            main, halo = list(main_u), list(halo_u)
            for sweep in range(SWEEPS - 1):
                keep, push = ratios[sweep]
                ends = sweep == SWEEPS - 2
                main_z = vertical(main)
                halo_z = None if ends else vertical(halo)
                for h in range(2):
                    main_next, main_prev = turn(main[h], -8), turn(main[h], 8)
                    halo_next, halo_prev = turn(halo[h], -8), turn(halo[h], 8)
                    total = main_s[h] + main_z[h]
                    total = total + main_out * jnp.where(last, halo_next, main_next)
                    total = total + main_in * jnp.where(first, halo_prev, main_prev)
                    main_u[h] = keep * main_u[h] + push * (total * main_invs[h] - main[h])
                    if not ends:
                        total = halo_s[h] + halo_z[h]
                        total = total + halo_out * jnp.where(last, main_next, halo_next)
                        total = total + halo_in * jnp.where(first, main_prev, halo_prev)
                        halo_u[h] = keep * halo_u[h] + push * (total * halo_invs[h] - halo[h])
                for h in range(2):
                    main[h] = main[h] + main_u[h]
                    if not ends:
                        halo[h] = halo[h] + halo_u[h]
            own_ref[pl.ds(at, 8), :] = jnp.where(inside < 4, turn(main[0], -4), turn(main[1], 4))

    own_high, own_low = halves(own_ref[...])
    both = jnp.concatenate([own_high, own_low], axis=1)
    step = 96
    for m in range(0, SECTORS * RANK, step):
        wide = dot(vh_ref[m : m + step, :], both)
        out_ref[m : m + step, :] = (
            wide[:, :LANES] + wide[:, LANES:] + dot(vl_ref[m : m + step, :], own_high)
        )


def expand_kernel(q_ref, stretch_ref, out_ref, y_ref):
    for c in range(0, RANK, 8):
        rows = swap_groups([q_ref[q, c : c + 8, :] for q in range(SECTORS)])
        for r in range(ROWS):
            y_ref[r, c : c + 8, :] = rows[r]
    stretch = stretch_ref[...]
    for r in range(0, ROWS, 2):
        columns = []
        for k in range(2):
            high, low = halves(y_ref[r + k])
            columns.append(jnp.concatenate([high, low, high, low], axis=0))
        wide = dot(stretch, jnp.concatenate(columns, axis=1))
        out_ref[r] = wide[:, :LANES]
        out_ref[r + 1] = wide[:, LANES:]


def call(kernel, outs, scratch, name, first_in_smem=False, count=1, **options):
    whole = pl.BlockSpec(memory_space=pltpu.VMEM)
    specs = [whole] * count
    if first_in_smem:
        specs[0] = pl.BlockSpec(memory_space=pltpu.SMEM)
    single = len(outs) == 1
    shapes = [jax.ShapeDtypeStruct(shape, F32) for shape in outs]
    return pl.pallas_call(
        kernel,
        out_shape=shapes[0] if single else shapes,
        in_specs=specs,
        out_specs=whole if single else [whole] * len(outs),
        scratch_shapes=[pltpu.VMEM(shape, F32) for shape in scratch],
        compiler_params=pltpu.CompilerParams(vmem_limit_bytes=40 * 1024 * 1024),
        name=name,
        **options,
    )


def compress(density, squeeze, **options):
    return call(
        compress_kernel,
        [(SECTORS, RANK, 2 * LANES)],
        [(ROWS, RANK, LANES)],
        "compress",
        count=2,
        **options,
    )(density, squeeze)


def make_source(received, high, low, **options):
    return call(
        source_kernel,
        [(COEFS, 2 * LANES), (MODES, LANES), (MODES, LANES)],
        [],
        "make_source",
        count=3,
        **options,
    )(received, high, low)


def solve(place, source, low, high, v_high, v_low, **options):
    return call(
        solve_kernel,
        [(SECTORS * RANK, LANES)],
        [(COEFS, LANES)],
        "solve",
        first_in_smem=True,
        count=6,
        **options,
    )(place, source, low, high, v_high, v_low)


def expand(received, stretch, **options):
    return call(
        expand_kernel,
        [(ROWS, SECTOR, DEPTH)],
        [(ROWS, RANK, LANES)],
        "expand",
        count=2,
        **options,
    )(received, stretch)


def per_device(density):
    squeeze, forward, inverse, stretch = (
        jax.tree.map(jnp.asarray, item) for item in tables()
    )
    count = lax.axis_size("rad")
    place = jnp.stack(
        [
            lax.axis_index("rad") * ROWS,
            jnp.int32(count * ROWS),
            lax.axis_index("azi") * GROUP,
        ]
    ).astype(jnp.int32)
    outgoing = compress(density, squeeze)
    received = lax.all_to_all(outgoing, "azi", 0, 0)
    received = received.reshape(SECTORS * RANK, 2 * LANES)
    source, down, up = make_source(received, *forward)
    low = lax.ppermute(up, "rad", [(i, i + 1) for i in range(count - 1)])
    high = lax.ppermute(down, "rad", [(i + 1, i) for i in range(count - 1)])
    solved = solve(place, source, low, high, *inverse)
    received = lax.all_to_all(solved.reshape(SECTORS, RANK, LANES), "azi", 0, 0)
    return expand(received, stretch)


def solution(mesh):
    spec = P("rad", "azi", None)
    return jax.shard_map(
        per_device, mesh=mesh, in_specs=(spec,), out_specs=spec, check_vma=False
    )
```

time: 218 us -> 65.7 us (0.30)
  the two profiles are of different devices: /device:TPU:1 before, /device:TPU:240 now
where the time goes in v1:
time: 65.7 us; the launch traced here: 65.3 us
  blocking collectives  31.5 us (48%)
  Pallas kernels  13.3 us (20%)
  waiting for transfers between devices  10.7 us (16%)
  starting transfers between devices  7.63 us (12%)
  local copies, waits for them, and re-layouts  2.05 us (3%)
    all_to_all x1, blocking collectives, per_device(): received = lax.all_to_all(outgoing, 'azi', 0, 0)  18.1 us
    all_to_all x1, blocking collectives, per_device(): received = lax.all_to_all(solved.reshape(SECTORS, RANK, LANES), 'azi', 0, 0)  13.4 us
    pallas_call x1, Pallas kernels, solve(): call(solve_kernel, [(SECTORS * RANK, LANES)], [(COEFS, LANES)], 'solve',...  9.84 us
    ppermute x1, waiting for transfers between devices, per_device(): high = lax.ppermute(down, 'rad', [(i + 1, i) for i in range(count - 1)])  7.82 us
    ppermute x1, starting transfers between devices, per_device(): low = lax.ppermute(up, 'rad', [(i, i + 1) for i in range(count - 1)])  5.71 us
    ppermute x1, waiting for transfers between devices, per_device(): low = lax.ppermute(up, 'rad', [(i, i + 1) for i in range(count - 1)])  2.83 us
    unnamed x14, local copies, waits for them, and re-layouts  2.05 us
    ppermute x1, starting transfers between devices, per_device(): high = lax.ppermute(down, 'rad', [(i + 1, i) for i in range(count - 1)])  1.92 us
  transfers between devices with their start and end apart: 2, of which 2 were waited for; matrix products, arithmetic and copies ran while one was open for 0% of the time, Pallas kernels for 0%

profile of v1, /device:TPU:240, one launch (start us, length us, event | category | flops | bytes accessed | tf_op | source)
XLA Modules:
  0.0 65.3 jit_solution(728166402817704799)
XLA Ops:
  0.0 0.0 copy-start
  0.0 1.2 %copy-done = f32[16,128,128]{2,1,0:T(8,128)S(1)} copy-done((f32[16,128,128]{2,1,0:T(8,128)S(1)}, f32[16,128,128]{2,1,0:T(8,128)}, u32[]{:S(2)}) %copy-start) | copy-done | bytes 1048600
  1.2 0.0 copy-start.6
  1.2 0.8 %copy-done.6 = bf16[96,256]{1,0:T(8,128)(2,1)S(1)} copy-done((bf16[96,256]{1,0:T(8,128)(2,1)S(1)}, bf16[96,256]{1,0:T(8,128)(2,1)}, u32[]{:S(2)}) %copy-start.6) | copy-done | bytes 49176
  2.0 0.8 %compress.1 = f32[16,48,256]{2,1,0:T(8,128)S(1)} custom-call(f32[16,128,128]{2,1,0:T(8,128)S(1)} %copy-done, bf16[96,256]{1,0:T(8,128)(2,1)S(1)} %copy-done.6), custom_call_target="tpu_custom_call" | custom-call | tf_op jit(solution)/shard_map/compress/pallas_call | solution.py:282
  2.9 0.0 copy-start.3
  2.9 0.0 copy-start.4
  2.9 18.1 %all_to_all.10 = f32[16,48,256]{2,1,0:T(8,128)S(1)} all-to-all(f32[16,48,256]{2,1,0:T(8,128)S(1)} %compress.1), channel_id=1, replica_groups=mesh['rad'=32,'azi'=16] {'azi'}, dimensions={0} | all-to-all | bytes 1572864 | tf_op jit(solution)/shard_map/all_to_all | solution.py:339
  21.0 0.0 copy-done.3
  21.0 0.0 copy-done.4
  21.0 0.0 copy-start.1
  21.0 0.0 copy-start.2
  21.0 1.0 %make_source.1 = (f32[512,256]{1,0:T(8,128)S(1)}, f32[256,128]{1,0:T(8,128)S(1)}, f32[256,128]{1,0:T(8,128)S(1)}) custom-call(f32[768,256]{1,0:T(8,128)S(1)} %bitcast.4, bf16[512,768]{1,0:T(8,128)(2,1)S(1)} %copy-done.3, bf16[512,768]{1,0:T(8,128)(2,1)S(1)} %copy-done.4), custom_call_target="tpu_custom_call" | custom-call | tf_op jit(solution)/shard_map/make_source/pallas_call | solution.py:293
  22.0 5.7 %collective-permute-start = (f32[256,128]{1,0:T(8,128)S(1)}, f32[256,128]{1,0:T(8,128)S(1)}, u32[]{:S(2)}, u32[]{:S(2)}) collective-permute-start(f32[256,128]{1,0:T(8,128)S(1)} %get-tuple-element.9), channel_id=1, source_target_pairs={{0,16},{16,32},{32,48},{48,64},{64,80},{80,96},{96,112},{112,128},... | collective-permute-start | bytes 393224 | tf_op jit(solution)/shard_map/ppermute | solution.py:342
  27.7 1.9 %collective-permute-start.1 = (f32[256,128]{1,0:T(8,128)S(1)}, f32[256,128]{1,0:T(8,128)S(1)}, u32[]{:S(2)}, u32[]{:S(2)}) collective-permute-start(f32[256,128]{1,0:T(8,128)S(1)} %get-tuple-element.10), channel_id=1, source_target_pairs={{16,0},{32,16},{48,32},{64,48},{80,64},{96,80},{112,96},{128,112},... | collective-permute-start | bytes 393224 | tf_op jit(solution)/shard_map/ppermute | solution.py:343
  29.6 0.1 pad_add_fusion.place_ref
  29.7 2.8 %collective-permute-done.low_ref = f32[256,128]{1,0:T(8,128)S(1)} collective-permute-done((f32[256,128]{1,0:T(8,128)S(1)}, f32[256,128]{1,0:T(8,128)S(1)}, u32[]{:S(2)}, u32[]{:S(2)}) %collective-permute-start) | collective-permute-done | bytes 131104 | tf_op jit(solution)/shard_map/ppermute | solution.py:342
  32.5 7.8 %collective-permute-done.1.high_ref = f32[256,128]{1,0:T(8,128)S(1)} collective-permute-done((f32[256,128]{1,0:T(8,128)S(1)}, f32[256,128]{1,0:T(8,128)S(1)}, u32[]{:S(2)}, u32[]{:S(2)}) %collective-permute-start.1) | collective-permute-done | bytes 131104 | tf_op jit(solution)/shard_map/ppermute | solution.py:343
  40.4 0.0 copy-done.1
  40.4 0.0 copy-done.2
  40.4 9.8 %solve.1 = f32[768,128]{1,0:T(8,128)S(1)} custom-call(s32[3]{0:T(128)S(1)} %pad_add_fusion.place_ref, f32[512,256]{1,0:T(8,128)S(1)} %get-tuple-element.8.s_ref, f32[256,128]{1,0:T(8,128)S(1)} %collective-permute-done.low_ref, f32[256,128]{1,0:T(8,128)S(1)} %collective-permute-done.1.high_ref, bf16[768,512]{1,0:T(8,128)(2,1)S(1)} %copy-done.1, ...), custom_call_target="tpu_custom_call" | custom-call | tf_op jit(solution)/shard_map/solve/pallas_call | solution.py:304
  50.2 0.0 copy-start.5
  50.2 13.4 %all_to_all.11.q_ref = f32[16,48,128]{2,1,0:T(8,128)S(1)} all-to-all(f32[16,48,128]{2,1,0:T(8,128)S(1)} %bitcast.5), channel_id=1, replica_groups=mesh['rad'=32,'azi'=16] {'azi'}, dimensions={0} | all-to-all | bytes 786432 | tf_op jit(solution)/shard_map/all_to_all | solution.py:345
  63.6 0.0 copy-done.5
  63.6 1.7 %expand.1 = f32[16,128,128]{2,1,0:T(8,128)} custom-call(f32[16,48,128]{2,1,0:T(8,128)S(1)} %all_to_all.11.q_ref, bf16[128,192]{1,0:T(8,128)(2,1)S(1)} %copy-done.5), custom_call_target="tpu_custom_call" | custom-call | tf_op jit(solution)/shard_map/expand/pallas_call | solution.py:316
Async XLA Ops:
  0.0 1.2 %copy-start = (f32[16,128,128]{2,1,0:T(8,128)S(1)}, f32[16,128,128]{2,1,0:T(8,128)}, u32[]{:S(2)}) copy-start(f32[16,128,128]{2,1,0:T(8,128)} %x_ref.1) | copy-start | bytes 3145732
  1.2 0.8 %copy-start.6 = (bf16[96,256]{1,0:T(8,128)(2,1)S(1)}, bf16[96,256]{1,0:T(8,128)(2,1)}, u32[]{:S(2)}) copy-start(bf16[96,256]{1,0:T(8,128)(2,1)} %constant.27.clone.squeeze_ref) | copy-start | bytes 147460
  2.9 18.2 %copy-start.3 = (bf16[512,768]{1,0:T(8,128)(2,1)S(1)}, bf16[512,768]{1,0:T(8,128)(2,1)}, u32[]{:S(2)}) copy-start(bf16[512,768]{1,0:T(8,128)(2,1)} %constant.28.clone.high_ref) | copy-start | bytes 2359300
  2.9 18.1 %copy-start.4 = (bf16[512,768]{1,0:T(8,128)(2,1)S(1)}, bf16[512,768]{1,0:T(8,128)(2,1)}, u32[]{:S(2)}) copy-start(bf16[512,768]{1,0:T(8,128)(2,1)} %constant.29.clone.low_ref) | copy-start | bytes 2359300
  21.0 19.4 %copy-start.1 = (bf16[768,512]{1,0:T(8,128)(2,1)S(1)}, bf16[768,512]{1,0:T(8,128)(2,1)}, u32[]{:S(2)}) copy-start(bf16[768,512]{1,0:T(8,128)(2,1)} %constant.30.clone.vh_ref) | copy-start | bytes 2359300
  21.0 19.4 %copy-start.2 = (bf16[768,512]{1,0:T(8,128)(2,1)S(1)}, bf16[768,512]{1,0:T(8,128)(2,1)}, u32[]{:S(2)}) copy-start(bf16[768,512]{1,0:T(8,128)(2,1)} %constant.31.clone.vl_ref) | copy-start | bytes 2359300
  22.0 10.6 %collective-permute-start = (f32[256,128]{1,0:T(8,128)S(1)}, f32[256,128]{1,0:T(8,128)S(1)}, u32[]{:S(2)}, u32[]{:S(2)}) collective-permute-start(f32[256,128]{1,0:T(8,128)S(1)} %get-tuple-element.9), channel_id=1, source_target_pairs={{0,16},{16,32},{32,48},{48,64},{64,80},{80,96},{96,112},{112,128},... | collective-permute-start | bytes 393224 | tf_op jit(solution)/shard_map/ppermute | solution.py:342
  27.7 12.7 %collective-permute-start.1 = (f32[256,128]{1,0:T(8,128)S(1)}, f32[256,128]{1,0:T(8,128)S(1)}, u32[]{:S(2)}, u32[]{:S(2)}) collective-permute-start(f32[256,128]{1,0:T(8,128)S(1)} %get-tuple-element.10), channel_id=1, source_target_pairs={{16,0},{32,16},{48,32},{64,48},{80,64},{96,80},{112,96},{128,112},... | collective-permute-start | bytes 393224 | tf_op jit(solution)/shard_map/ppermute | solution.py:343
  50.2 13.4 %copy-start.5 = (bf16[128,192]{1,0:T(8,128)(2,1)S(1)}, bf16[128,192]{1,0:T(8,128)(2,1)}, u32[]{:S(2)}) copy-start(bf16[128,192]{1,0:T(8,128)(2,1)} %constant.32.clone.stretch_ref) | copy-start | bytes 147460

commit v2 on v1

v2 whole, which is shorter than its diff:
```python
import functools
import math

import jax
import jax.numpy as jnp
import numpy as np
from jax import lax
from jax.experimental import pallas as pl
from jax.experimental.pallas import tpu as pltpu
from jax.sharding import PartitionSpec as P

NPHI = 2048
MODES = 256
SWEEPS = 4
SECTORS = 16
SECTOR = NPHI // SECTORS
COEFS = 2 * MODES
RANK = 48
ROWS = 16
DEPTH = 128
GROUP = 8
LANES = 128
HALF = RANK // 2
BLOCKS = 8
BLOCK_ROWS = 8
EXTENDED = BLOCK_ROWS + 6
CELLS = 3 * GROUP * BLOCK_ROWS
CHUNKS = 4

low_bound = 0.1
high_bound = 2.0
theta = 0.5 * (high_bound + low_bound)
delta = 0.5 * (high_bound - low_bound)
sigma = theta / delta
four_pi = 4.0 * math.pi

BF = jnp.bfloat16
F32 = jnp.float32


def split_table(table):
    high = table.astype(np.float32).astype(BF)
    low = (table - high.astype(np.float64)).astype(np.float32).astype(BF)
    return high, low


@functools.cache
def tables():
    modes = np.arange(MODES)
    angle = 2.0 * np.pi * ((np.arange(SECTOR)[:, None] * modes[None, :]) % NPHI) / NPHI
    first = np.concatenate([np.cos(angle), np.sin(angle)], axis=1)
    left, _, _ = np.linalg.svd(first, full_matrices=False)
    left = left[:, :RANK]
    cores = []
    for sector in range(SECTORS):
        cells = sector * SECTOR + np.arange(SECTOR)
        angle = 2.0 * np.pi * ((cells[:, None] * modes[None, :]) % NPHI) / NPHI
        cores.append(left.T @ np.concatenate([np.cos(angle), np.sin(angle)], axis=1))
    core = np.concatenate(cores, axis=0)
    weight = np.where(np.tile(modes, 2) == 0, 1.0, 2.0)
    left_high, left_low = split_table(left)
    ordered = core.reshape(SECTORS, 2, HALF, COEFS).transpose(1, 0, 2, 3)
    forward = split_table(ordered.reshape(SECTORS * RANK, COEFS) * (-four_pi / NPHI))
    inverse = split_table(core * weight[None, :])
    squeeze = np.concatenate(
        [
            np.concatenate([left_high.T, left_high.T], axis=1),
            np.concatenate([left_low.T, left_low.T], axis=1),
        ],
        axis=0,
    )
    stretch = np.concatenate([left_high, left_high, left_low, left_low], axis=1)
    return squeeze, forward, inverse, stretch


def halves(value):
    high = value.astype(BF)
    low = (value - high.astype(F32)).astype(BF)
    return high, low


def dot(a, b):
    return jnp.dot(a, b, preferred_element_type=F32)


def swap_groups(blocks, size):
    blocks = list(blocks)
    group = lax.broadcasted_iota(jnp.int32, blocks[0].shape, 1) // size
    bit = 1
    while bit < len(blocks):
        keep = (group & bit) == 0
        for i in range(len(blocks)):
            if i & bit:
                continue
            j = i | bit
            one, two = blocks[i], blocks[j]
            blocks[i] = jnp.where(keep, one, pltpu.roll(two, size * bit, 1))
            blocks[j] = jnp.where(keep, pltpu.roll(one, LANES - size * bit, 1), two)
        bit *= 2
    return blocks


def compress_kernel(x_hbm, squeeze_hbm, out_ref, x_ref, squeeze_ref, y_ref, sems):
    table_copy = pltpu.make_async_copy(squeeze_hbm, squeeze_ref, sems.at[CHUNKS])
    table_copy.start()
    rows = ROWS // CHUNKS
    copies = []
    for k in range(CHUNKS):
        part = pl.ds(k * rows, rows)
        copies.append(pltpu.make_async_copy(x_hbm.at[part], x_ref.at[part], sems.at[k]))
        copies[-1].start()
    table_copy.wait()
    squeeze = squeeze_ref[...]
    for r in range(0, ROWS, 2):
        if r % rows == 0:
            copies[r // rows].wait()
        columns = []
        for k in range(2):
            columns.append(jnp.concatenate(halves(x_ref[r + k]), axis=0))
        y = dot(squeeze, jnp.concatenate(columns, axis=1))
        y = y[:RANK] + y[RANK:]
        y_ref[r] = y[:, :LANES]
        y_ref[r + 1] = y[:, LANES:]
    lane = lax.broadcasted_iota(jnp.int32, (8, LANES), 1)
    inside = lane % GROUP
    for c in range(0, HALF, 8):
        pair = []
        for start in (c, c + HALF):
            groups = swap_groups(
                [pltpu.roll(y_ref[r, start : start + 8, :], 4, 1) for r in range(ROWS)], GROUP
            )
            edge = groups[0]
            groups[0] = jnp.where(inside >= 4, edge, 0.0)
            groups.append(jnp.where(inside < 4, edge, 0.0))
            pair.append(groups)
        for g in range(2 * BLOCKS + 1):
            one, two = pair[0][g], pair[1][g]
            packed = (
                jnp.where(lane < 64, one, pltpu.roll(two, 64, 1)),
                jnp.where(lane < 64, pltpu.roll(one, 64, 1), two),
            )
            for j in range(3):
                if (g - j) % 2 or not 0 <= (g - j) // 2 < BLOCKS:
                    continue
                for side in range(2):
                    at = j * HALF + c
                    out_ref[g - j + side, at : at + 8, :] = packed[side]


def source_kernel(p_ref, high_ref, low_ref, s_ref, down_ref, up_ref):
    turned = []
    for j in range(3):
        block = p_ref[:, j * HALF : (j + 1) * HALF, :].reshape(SECTORS * HALF, LANES).T
        turned.append(jnp.concatenate([block[:64], block[64:]], axis=1))
    cells_high, cells_low = halves(jnp.concatenate(turned, axis=0))
    both = jnp.concatenate([cells_high, cells_low], axis=0)
    for n in range(0, COEFS, 256):
        wide = dot(both, high_ref[:, n : n + 256])
        s_ref[:, n : n + 256] = (
            wide[:CELLS] + wide[CELLS:] + dot(cells_high, low_ref[:, n : n + 256])
        )
    level = lax.broadcasted_iota(jnp.int32, (8, COEFS), 0)

    def at(j, r):
        start = j * 64 + r * 8
        return s_ref[start : start + 8, :]

    for ref, (near, middle, far) in ((down_ref, (0, 1, 2)), (up_ref, (7, 6, 5))):
        ref[0:8, :] = jnp.where(level < 4, at(2, far), at(0, far))
        ref[8:16, :] = jnp.where(level < 2, pltpu.roll(at(2, middle), 5, 0), at(0, near))
        ref[16:24, :] = at(2, near)
        ref[24:32, :] = jnp.where(level < 3, at(2, middle), at(0, middle))
        ref[32:40, :] = at(1, near)
        ref[40:48, :] = at(1, middle)
        ref[48:56, :] = at(1, far)


def solve_kernel(
    place_ref, s_ref, low_ref, high_ref, vh_ref, vl_ref, out_ref, inverse_ref, weight_ref, own_ref
):
    shape = (8, LANES)
    level = lax.broadcasted_iota(jnp.int32, shape, 0)
    lane = lax.broadcasted_iota(jnp.int32, shape, 1)
    row_first = place_ref[0]
    row_count = place_ref[1]
    depth_first = place_ref[2]
    bottom = jnp.where(depth_first - 4 + level >= 0, 1.0, 0.0).astype(F32)
    top = jnp.where(depth_first + 12 + level < DEPTH, 1.0, 0.0).astype(F32)

    for e in range(EXTENDED):
        row = jnp.full(shape, row_first + (e - 3), jnp.int32)
        inverse = 1.0 / (row.astype(F32) + 0.5)
        weight_ref[e, 0] = 1.0 + 0.5 * inverse
        weight_ref[e, 1] = 1.0 - 0.5 * inverse
        good = jnp.where((row >= 0) & (row < row_count), 1.0, 0.0).astype(F32)
        for t in range(2):
            ratio = (lane + t * LANES).astype(F32) * inverse
            inverse_ref[t, e] = good / (4.0 + ratio * ratio)

    def turn(value, amount):
        return pltpu.roll(value, amount % 8, 0)

    ratios = []
    ratio = 1.0 / sigma
    for _ in range(SWEEPS - 1):
        following = 1.0 / (2.0 * sigma - ratio)
        ratios.append((following * ratio, 2.0 * following / delta))
        ratio = following

    @pl.loop(0, 4)
    def _(tile):
        lanes = pl.ds(pl.multiple_of(tile * LANES, LANES), LANES)
        table = tile % 2

        def load(ref, start):
            return ref[start : start + 8, lanes]

        def halo(ref, distance):
            if distance == 3:
                both = load(ref, 0)
                return [both, load(ref, 48), both]
            if distance == 2:
                both = load(ref, 24)
                rest = turn(load(ref, 8), 3)
                return [both, load(ref, 40), jnp.where(level < 3, both, rest)]
            return [load(ref, 8), load(ref, 32), load(ref, 16)]

        def source(e):
            if e < 3:
                return halo(low_ref, 3 - e)
            if e >= 11:
                return halo(high_ref, e - 10)
            return [load(s_ref, j * 64 + (e - 3) * 8) for j in range(3)]

        given, scale, step = {}, {}, {}
        state = [{} for _ in range(SWEEPS)]
        for newest in range(EXTENDED + SWEEPS - 1):
            e = newest
            if e < EXTENDED:
                given[e] = source(e)
                middle = inverse_ref[table, e]
                scale[e] = [middle * bottom, middle, middle * top]
                step[e] = [g * i * (1.0 / theta) for g, i in zip(given[e], scale[e])]
                state[0][e] = step[e]
            for sweep in range(1, SWEEPS):
                e = newest - sweep
                if not sweep <= e < EXTENDED - sweep:
                    continue
                keep, push = ratios[sweep - 1]
                old = state[sweep - 1]
                center, outer, inner = old[e], old[e + 1], old[e - 1]
                out_weight, in_weight = weight_ref[e, 0], weight_ref[e, 1]
                above = [turn(x, -1) for x in center]
                below = [turn(x, 1) for x in center]
                steps, values = [], []
                for j in range(3):
                    higher = above[j]
                    if j < 2:
                        higher = jnp.where(level == 7, above[j + 1], higher)
                    lower = below[j]
                    if j > 0:
                        lower = jnp.where(level == 0, below[j - 1], lower)
                    total = given[e][j] + (higher + lower)
                    total = total + (out_weight * outer[j] + in_weight * inner[j])
                    move = keep * step[e][j] + push * (total * scale[e][j] - center[j])
                    steps.append(move)
                    values.append(center[j] + move)
                step[e] = steps
                state[sweep][e] = values
            e = newest - (SWEEPS - 1)
            if 3 <= e < 11:
                x = state[SWEEPS - 1][e]
                at = (e - 3) * 16
                own_ref[at : at + 8, lanes] = turn(jnp.where(level < 4, x[1], x[0]), 4)
                own_ref[at + 8 : at + 16, lanes] = turn(jnp.where(level < 4, x[2], x[1]), 4)

    own_high, own_low = halves(own_ref[...])
    both = jnp.concatenate([own_high, own_low], axis=0)

    def across(a, b):
        return lax.dot_general(a, b, (((1,), (1,)), ((), ())), preferred_element_type=F32)

    step_rows = 192
    for m in range(0, SECTORS * RANK, step_rows):
        wide = across(vh_ref[m : m + step_rows, :], both)
        out_ref[m : m + step_rows, :] = (
            wide[:, :LANES]
            + wide[:, LANES:]
            + across(vl_ref[m : m + step_rows, :], own_high)
        )


def expand_kernel(q_ref, stretch_ref, out_hbm, y_ref, out_ref, sems):
    for side in range(2):
        for c in range(0, RANK, 8):
            rows = swap_groups(
                [q_ref[2 * b + side, c : c + 8, :] for b in range(BLOCKS)], 2 * GROUP
            )
            for r in range(BLOCK_ROWS):
                y_ref[side * BLOCK_ROWS + r, c : c + 8, :] = rows[r]
    stretch = stretch_ref[...]
    rows = ROWS // CHUNKS
    copies = []
    for r in range(0, ROWS, 2):
        columns = []
        for k in range(2):
            high, low = halves(y_ref[r + k])
            columns.append(jnp.concatenate([high, low, high, low], axis=0))
        wide = dot(stretch, jnp.concatenate(columns, axis=1))
        out_ref[r] = wide[:, :LANES]
        out_ref[r + 1] = wide[:, LANES:]
        if (r + 2) % rows == 0:
            part = pl.ds(r + 2 - rows, rows)
            copies.append(
                pltpu.make_async_copy(out_ref.at[part], out_hbm.at[part], sems.at[len(copies)])
            )
            copies[-1].start()
    for copy in copies:
        copy.wait()


VMEM = pl.BlockSpec(memory_space=pltpu.VMEM)
SMEM = pl.BlockSpec(memory_space=pltpu.SMEM)
HBM = pl.BlockSpec(memory_space=pltpu.HBM)


def call(kernel, outs, in_specs, scratch, name, out_space=VMEM, **options):
    single = len(outs) == 1
    shapes = [jax.ShapeDtypeStruct(shape, F32) for shape in outs]
    return pl.pallas_call(
        kernel,
        out_shape=shapes[0] if single else shapes,
        in_specs=in_specs,
        out_specs=out_space if single else [out_space] * len(outs),
        scratch_shapes=scratch,
        compiler_params=pltpu.CompilerParams(vmem_limit_bytes=40 * 1024 * 1024),
        name=name,
        **options,
    )


def compress(density, squeeze, **options):
    return call(
        compress_kernel,
        [(SECTORS, 3 * HALF, LANES)],
        [HBM, HBM],
        [
            pltpu.VMEM((ROWS, SECTOR, DEPTH), F32),
            pltpu.VMEM((2 * RANK, 2 * SECTOR), BF),
            pltpu.VMEM((ROWS, RANK, LANES), F32),
            pltpu.SemaphoreType.DMA((CHUNKS + 1,)),
        ],
        "compress",
        **options,
    )(density, squeeze)


def make_source(received, high, low, **options):
    return call(
        source_kernel,
        [(CELLS, COEFS), (56, COEFS), (56, COEFS)],
        [VMEM] * 3,
        [],
        "make_source",
        **options,
    )(received, high, low)


def solve(place, source, low, high, v_high, v_low, **options):
    return call(
        solve_kernel,
        [(SECTORS * RANK, LANES)],
        [SMEM] + [VMEM] * 5,
        [
            pltpu.VMEM((2, EXTENDED, 8, LANES), F32),
            pltpu.VMEM((EXTENDED, 2, 8, LANES), F32),
            pltpu.VMEM((LANES, COEFS), F32),
        ],
        "solve",
        **options,
    )(place, source, low, high, v_high, v_low)


def expand(received, stretch, **options):
    return call(
        expand_kernel,
        [(ROWS, SECTOR, DEPTH)],
        [VMEM] * 2,
        [
            pltpu.VMEM((ROWS, RANK, LANES), F32),
            pltpu.VMEM((ROWS, SECTOR, DEPTH), F32),
            pltpu.SemaphoreType.DMA((CHUNKS,)),
        ],
        "expand",
        out_space=HBM,
        **options,
    )(received, stretch)


def per_device(density):
    squeeze, forward, inverse, stretch = (
        jax.tree.map(jnp.asarray, item) for item in tables()
    )
    count = lax.axis_size("rad")
    azi = lax.axis_index("azi")
    place = jnp.stack(
        [
            lax.axis_index("rad") * ROWS + azi % 2 * BLOCK_ROWS,
            jnp.int32(count * ROWS),
            azi // 2 * 2 * GROUP,
        ]
    ).astype(jnp.int32)
    outgoing = compress(density, squeeze)
    received = lax.all_to_all(outgoing, "azi", 0, 0)
    source, down, up = make_source(received, *forward)
    outward = []
    for device in range(count * SECTORS):
        target = device + (1 if device % 2 == 0 else SECTORS - 1)
        if target < count * SECTORS:
            outward.append((device, target))
    axes = ("rad", "azi")
    low = lax.ppermute(up, axes, outward)
    high = lax.ppermute(down, axes, [(target, device) for device, target in outward])
    solved = solve(place, source, low, high, *inverse)
    received = lax.all_to_all(solved.reshape(SECTORS, RANK, LANES), "azi", 0, 0)
    return expand(received, stretch)


def solution(mesh):
    spec = P("rad", "azi", None)
    return jax.shard_map(
        per_device, mesh=mesh, in_specs=(spec,), out_specs=spec, check_vma=False
    )
```

time: 65.7 us -> 53.8 us (0.82)
  waiting for transfers between devices: 10.7 us -> 3.46 us
  Pallas kernels: 13.3 us -> 6.33 us
  blocking collectives: 31.5 us -> 35 us
  starting transfers between devices: 7.63 us -> 6.46 us
    ppermute x2, waiting for transfers between devices: 10.7 us -> 3.46 us  [the longest x1 2.93 us: per_device(): lax.ppermute(down, axes, [(target, device) for device, target in outward])]
    pallas_call x4, Pallas kernels: 13.3 us -> 6.33 us  [the longest x1 2.29 us: solve(): call(solve_kernel, [(SECTORS * RANK, LANES)], [SMEM] + [VMEM] * 5, [pltpu...]
    all_to_all x1, blocking collectives: 13.4 us -> 19 us  [per_device(): received = lax.all_to_all(solved.reshape(SECTORS, RANK, LANES), 'azi', 0, 0)]
    all_to_all x1, blocking collectives: 18.1 us -> 16 us  [per_device(): received = lax.all_to_all(outgoing, 'azi', 0, 0)]
    ppermute x2, starting transfers between devices: 7.63 us -> 6.46 us  [the longest x1 4.48 us: per_device(): lax.ppermute(down, axes, [(target, device) for device, target in outward])]
where the time goes in v2:
time: 53.8 us; the launch traced here: 53.5 us
  blocking collectives  35 us (65%)
  starting transfers between devices  6.46 us (12%)
  Pallas kernels  6.33 us (12%)
  waiting for transfers between devices  3.46 us (6%)
  local copies, waits for them, and re-layouts  2.05 us (4%)
    all_to_all x1, blocking collectives, per_device(): received = lax.all_to_all(solved.reshape(SECTORS, RANK, LANES), 'azi', 0, 0)  19 us
    all_to_all x1, blocking collectives, per_device(): received = lax.all_to_all(outgoing, 'azi', 0, 0)  16 us
    ppermute x1, starting transfers between devices, per_device(): lax.ppermute(down, axes, [(target, device) for device, target in outward])  4.48 us
    ppermute x1, waiting for transfers between devices, per_device(): lax.ppermute(down, axes, [(target, device) for device, target in outward])  2.93 us
    pallas_call x1, Pallas kernels, solve(): call(solve_kernel, [(SECTORS * RANK, LANES)], [SMEM] + [VMEM] * 5, [pltpu...  2.29 us
    unnamed x14, local copies, waits for them, and re-layouts  2.05 us
    ppermute x1, starting transfers between devices, per_device(): low = lax.ppermute(up, axes, outward)  1.98 us
    pallas_call x1, Pallas kernels, compress(): call(compress_kernel, [(SECTORS, 3 * HALF, LANES)], [HBM, HBM], [pltpu.VM...  1.86 us
  transfers between devices with their start and end apart: 2, of which 2 were waited for; matrix products, arithmetic and copies ran while one was open for 0% of the time, Pallas kernels for 0%

profile of v2, /device:TPU:240, one launch (start us, length us, event | category | flops | bytes accessed | tf_op | source)
XLA Modules:
  0.0 53.5 jit_solution(6557128781521791661)
XLA Ops:
  0.0 0.0 copy-start
  0.0 1.2 %copy-done = f32[16,128,128]{2,1,0:T(8,128)S(1)} copy-done((f32[16,128,128]{2,1,0:T(8,128)S(1)}, f32[16,128,128]{2,1,0:T(8,128)}, u32[]{:S(2)}) %copy-start) | copy-done | bytes 1048600
  1.2 0.0 copy-start.6
  1.2 0.8 %copy-done.6 = bf16[96,256]{1,0:T(8,128)(2,1)S(1)} copy-done((bf16[96,256]{1,0:T(8,128)(2,1)S(1)}, bf16[96,256]{1,0:T(8,128)(2,1)}, u32[]{:S(2)}) %copy-start.6) | copy-done | bytes 49176
  2.0 0.0 copy-start.2
  2.0 1.9 %compress.1 = f32[16,72,128]{2,1,0:T(8,128)S(1)} custom-call(f32[16,128,128]{2,1,0:T(8,128)S(1)} %copy-done, bf16[96,256]{1,0:T(8,128)(2,1)S(1)} %copy-done.6), custom_call_target="tpu_custom_call" | custom-call | tf_op jit(solution)/shard_map/compress/pallas_call | solution.py:343
  3.9 0.0 copy-start.1
  3.9 16.0 %all_to_all.10.p_ref = f32[16,72,128]{2,1,0:T(8,128)S(1)} all-to-all(f32[16,72,128]{2,1,0:T(8,128)S(1)} %compress.1), channel_id=1, replica_groups=mesh['rad'=32,'azi'=16] {'azi'}, dimensions={0} | all-to-all | bytes 1179648 | tf_op jit(solution)/shard_map/all_to_all | solution.py:414
  20.0 0.0 copy-done.2
  20.0 0.0 copy-done.1
  20.0 0.0 copy-start.3
  20.0 0.0 copy-start.4
  20.0 0.7 %make_source.1 = (f32[192,512]{1,0:T(8,128)S(1)}, f32[56,512]{1,0:T(8,128)S(1)}, f32[56,512]{1,0:T(8,128)S(1)}) custom-call(f32[16,72,128]{2,1,0:T(8,128)S(1)} %all_to_all.10.p_ref, bf16[768,512]{1,0:T(8,128)(2,1)S(1)} %copy-done.2, bf16[768,512]{1,0:T(8,128)(2,1)S(1)} %copy-done.1), custom_call_target="tpu_custom_call" | custom-call | tf_op jit(solution)/shard_map/make_source/pallas_call | solution.py:359
  20.7 2.0 %collective-permute-start = (f32[56,512]{1,0:T(8,128)S(1)}, f32[56,512]{1,0:T(8,128)S(1)}, u32[]{:S(2)}, u32[]{:S(2)}) collective-permute-start(f32[56,512]{1,0:T(8,128)S(1)} %get-tuple-element.9), channel_id=1, source_target_pairs={{0,1},{1,16},{2,3},{3,18},{4,5},{5,20},{6,7},{7,22},{8,9},{9,24},{... | collective-permute-start | bytes 344072 | tf_op jit(solution)/shard_map/ppermute | solution.py:422
  22.7 4.5 %collective-permute-start.1 = (f32[56,512]{1,0:T(8,128)S(1)}, f32[56,512]{1,0:T(8,128)S(1)}, u32[]{:S(2)}, u32[]{:S(2)}) collective-permute-start(f32[56,512]{1,0:T(8,128)S(1)} %get-tuple-element.10), channel_id=1, source_target_pairs={{1,0},{16,1},{3,2},{18,3},{5,4},{20,5},{7,6},{22,7},{9,8},{24,9},{... | collective-permute-start | bytes 344072 | tf_op jit(solution)/shard_map/ppermute | solution.py:423
  27.2 0.1 pad_add_fusion.place_ref
  27.3 0.5 %collective-permute-done.low_ref = f32[56,512]{1,0:T(8,128)S(1)} collective-permute-done((f32[56,512]{1,0:T(8,128)S(1)}, f32[56,512]{1,0:T(8,128)S(1)}, u32[]{:S(2)}, u32[]{:S(2)}) %collective-permute-start) | collective-permute-done | bytes 114720 | tf_op jit(solution)/shard_map/ppermute | solution.py:422
  27.8 2.9 %collective-permute-done.1.high_ref = f32[56,512]{1,0:T(8,128)S(1)} collective-permute-done((f32[56,512]{1,0:T(8,128)S(1)}, f32[56,512]{1,0:T(8,128)S(1)}, u32[]{:S(2)}, u32[]{:S(2)}) %collective-permute-start.1) | collective-permute-done | bytes 114720 | tf_op jit(solution)/shard_map/ppermute | solution.py:423
  30.7 0.0 copy-done.3
  30.7 0.0 copy-done.4
  30.7 2.3 %solve.1 = f32[768,128]{1,0:T(8,128)S(1)} custom-call(s32[3]{0:T(128)S(1)} %pad_add_fusion.place_ref, f32[192,512]{1,0:T(8,128)S(1)} %get-tuple-element.8.s_ref, f32[56,512]{1,0:T(8,128)S(1)} %collective-permute-done.low_ref, f32[56,512]{1,0:T(8,128)S(1)} %collective-permute-done.1.high_ref, bf16[768,512]{1,0:T(8,128)(2,1)S(1)} %copy-done.4, ...), custom_call_target="tpu_custom_call" | custom-call | tf_op jit(solution)/shard_map/solve/pallas_call | solution.py:370
  33.0 0.0 copy-start.5
  33.1 19.0 %all_to_all.11.q_ref = f32[16,48,128]{2,1,0:T(8,128)S(1)} all-to-all(f32[16,48,128]{2,1,0:T(8,128)S(1)} %bitcast.3), channel_id=1, replica_groups=mesh['rad'=32,'azi'=16] {'azi'}, dimensions={0} | all-to-all | bytes 786432 | tf_op jit(solution)/shard_map/all_to_all | solution.py:425
  52.0 0.0 copy-done.5
  52.0 1.5 %expand.1 = f32[16,128,128]{2,1,0:T(8,128)} custom-call(f32[16,48,128]{2,1,0:T(8,128)S(1)} %all_to_all.11.q_ref, bf16[128,192]{1,0:T(8,128)(2,1)S(1)} %copy-done.5), custom_call_target="tpu_custom_call" | custom-call | tf_op jit(solution)/shard_map/expand/pallas_call | solution.py:385
Async XLA Ops:
  0.0 1.2 %copy-start = (f32[16,128,128]{2,1,0:T(8,128)S(1)}, f32[16,128,128]{2,1,0:T(8,128)}, u32[]{:S(2)}) copy-start(f32[16,128,128]{2,1,0:T(8,128)} %x_hbm.1) | copy-start | bytes 3145732
  1.2 0.8 %copy-start.6 = (bf16[96,256]{1,0:T(8,128)(2,1)S(1)}, bf16[96,256]{1,0:T(8,128)(2,1)}, u32[]{:S(2)}) copy-start(bf16[96,256]{1,0:T(8,128)(2,1)} %constant.52.clone.squeeze_hbm) | copy-start | bytes 147460
  2.0 17.9 %copy-start.2 = (bf16[768,512]{1,0:T(8,128)(2,1)S(1)}, bf16[768,512]{1,0:T(8,128)(2,1)}, u32[]{:S(2)}) copy-start(bf16[768,512]{1,0:T(8,128)(2,1)} %constant.53.clone.high_ref) | copy-start | bytes 2359300
  3.9 16.1 %copy-start.1 = (bf16[768,512]{1,0:T(8,128)(2,1)S(1)}, bf16[768,512]{1,0:T(8,128)(2,1)}, u32[]{:S(2)}) copy-start(bf16[768,512]{1,0:T(8,128)(2,1)} %constant.54.clone.low_ref) | copy-start | bytes 2359300
  20.0 10.8 %copy-start.3 = (bf16[768,512]{1,0:T(8,128)(2,1)S(1)}, bf16[768,512]{1,0:T(8,128)(2,1)}, u32[]{:S(2)}) copy-start(bf16[768,512]{1,0:T(8,128)(2,1)} %constant.56.clone.vl_ref) | copy-start | bytes 2359300
  20.0 10.8 %copy-start.4 = (bf16[768,512]{1,0:T(8,128)(2,1)S(1)}, bf16[768,512]{1,0:T(8,128)(2,1)}, u32[]{:S(2)}) copy-start(bf16[768,512]{1,0:T(8,128)(2,1)} %constant.55.clone.vh_ref) | copy-start | bytes 2359300
  20.7 7.1 %collective-permute-start = (f32[56,512]{1,0:T(8,128)S(1)}, f32[56,512]{1,0:T(8,128)S(1)}, u32[]{:S(2)}, u32[]{:S(2)}) collective-permute-start(f32[56,512]{1,0:T(8,128)S(1)} %get-tuple-element.9), channel_id=1, source_target_pairs={{0,1},{1,16},{2,3},{3,18},{4,5},{5,20},{6,7},{7,22},{8,9},{9,24},{... | collective-permute-start | bytes 344072 | tf_op jit(solution)/shard_map/ppermute | solution.py:422
  22.7 8.1 %collective-permute-start.1 = (f32[56,512]{1,0:T(8,128)S(1)}, f32[56,512]{1,0:T(8,128)S(1)}, u32[]{:S(2)}, u32[]{:S(2)}) collective-permute-start(f32[56,512]{1,0:T(8,128)S(1)} %get-tuple-element.10), channel_id=1, source_target_pairs={{1,0},{16,1},{3,2},{18,3},{5,4},{20,5},{7,6},{22,7},{9,8},{24,9},{... | collective-permute-start | bytes 344072 | tf_op jit(solution)/shard_map/ppermute | solution.py:423
  33.0 19.0 %copy-start.5 = (bf16[128,192]{1,0:T(8,128)(2,1)S(1)}, bf16[128,192]{1,0:T(8,128)(2,1)}, u32[]{:S(2)}) copy-start(bf16[128,192]{1,0:T(8,128)(2,1)} %constant.57.clone.stretch_ref) | copy-start | bytes 147460

commit v3 on v2

--- a/solution.py
+++ b/solution.py
@@ -147,7 +147,7 @@
                     out_ref[g - j + side, at : at + 8, :] = packed[side]
 
 
-def source_kernel(p_ref, high_ref, low_ref, s_ref, down_ref, up_ref):
+def source_kernel(place_ref, p_ref, high_ref, low_ref, s_ref, cross_ref, chip_ref):
     turned = []
     for j in range(3):
         block = p_ref[:, j * HALF : (j + 1) * HALF, :].reshape(SECTORS * HALF, LANES).T
@@ -165,7 +165,7 @@
         start = j * 64 + r * 8
         return s_ref[start : start + 8, :]
 
-    for ref, (near, middle, far) in ((down_ref, (0, 1, 2)), (up_ref, (7, 6, 5))):
+    def pack(ref, near, middle, far):
         ref[0:8, :] = jnp.where(level < 4, at(2, far), at(0, far))
         ref[8:16, :] = jnp.where(level < 2, pltpu.roll(at(2, middle), 5, 0), at(0, near))
         ref[16:24, :] = at(2, near)
@@ -174,10 +174,36 @@
         ref[40:48, :] = at(1, middle)
         ref[48:56, :] = at(1, far)
 
+    core = place_ref[3]
+
+    @pl.when(core == 0)
+    def _():
+        pack(cross_ref, 0, 1, 2)
+        pack(chip_ref, 7, 6, 5)
+
+    @pl.when(core == 1)
+    def _():
+        pack(cross_ref, 7, 6, 5)
+        pack(chip_ref, 0, 1, 2)
+
 
 def solve_kernel(
-    place_ref, s_ref, low_ref, high_ref, vh_ref, vl_ref, out_ref, inverse_ref, weight_ref, own_ref
+    place_ref,
+    s_ref,
+    cross_ref,
+    chip_ref,
+    vh_ref,
+    vl_ref,
+    out_ref,
+    inverse_ref,
+    weight_ref,
+    own_ref,
+    low_ref,
+    high_ref,
 ):
+    core = place_ref[3]
+    low_ref[...] = jnp.where(core == 0, cross_ref[...], chip_ref[...])
+    high_ref[...] = jnp.where(core == 0, chip_ref[...], cross_ref[...])
     shape = (8, LANES)
     level = lax.broadcasted_iota(jnp.int32, shape, 0)
     lane = lax.broadcasted_iota(jnp.int32, shape, 1)
@@ -324,7 +350,7 @@
 HBM = pl.BlockSpec(memory_space=pltpu.HBM)
 
 
-def call(kernel, outs, in_specs, scratch, name, out_space=VMEM, **options):
+def call(kernel, outs, in_specs, scratch, name, out_space=VMEM, grant=40, **options):
     single = len(outs) == 1
     shapes = [jax.ShapeDtypeStruct(shape, F32) for shape in outs]
     return pl.pallas_call(
@@ -333,7 +359,7 @@
         in_specs=in_specs,
         out_specs=out_space if single else [out_space] * len(outs),
         scratch_shapes=scratch,
-        compiler_params=pltpu.CompilerParams(vmem_limit_bytes=40 * 1024 * 1024),
+        compiler_params=pltpu.CompilerParams(vmem_limit_bytes=grant * 1024 * 1024),
         name=name,
         **options,
     )
@@ -351,22 +377,23 @@
             pltpu.SemaphoreType.DMA((CHUNKS + 1,)),
         ],
         "compress",
+        grant=62,
         **options,
     )(density, squeeze)
 
 
-def make_source(received, high, low, **options):
+def make_source(place, received, high, low, **options):
     return call(
         source_kernel,
         [(CELLS, COEFS), (56, COEFS), (56, COEFS)],
-        [VMEM] * 3,
+        [SMEM] + [VMEM] * 3,
         [],
         "make_source",
         **options,
-    )(received, high, low)
-
-
-def solve(place, source, low, high, v_high, v_low, **options):
+    )(place, received, high, low)
+
+
+def solve(place, source, cross, chip, v_high, v_low, **options):
     return call(
         solve_kernel,
         [(SECTORS * RANK, LANES)],
@@ -375,10 +402,12 @@
             pltpu.VMEM((2, EXTENDED, 8, LANES), F32),
             pltpu.VMEM((EXTENDED, 2, 8, LANES), F32),
             pltpu.VMEM((LANES, COEFS), F32),
+            pltpu.VMEM((56, COEFS), F32),
+            pltpu.VMEM((56, COEFS), F32),
         ],
         "solve",
         **options,
-    )(place, source, low, high, v_high, v_low)
+    )(place, source, cross, chip, v_high, v_low)
 
 
 def expand(received, stretch, **options):
@@ -403,25 +432,24 @@
     )
     count = lax.axis_size("rad")
     azi = lax.axis_index("azi")
+    core = azi & 1
     place = jnp.stack(
         [
-            lax.axis_index("rad") * ROWS + azi % 2 * BLOCK_ROWS,
+            lax.axis_index("rad") * ROWS + core * BLOCK_ROWS,
             jnp.int32(count * ROWS),
-            azi // 2 * 2 * GROUP,
+            (azi >> 1) * 2 * GROUP,
+            core,
         ]
     ).astype(jnp.int32)
     outgoing = compress(density, squeeze)
     received = lax.all_to_all(outgoing, "azi", 0, 0)
-    source, down, up = make_source(received, *forward)
-    outward = []
-    for device in range(count * SECTORS):
-        target = device + (1 if device % 2 == 0 else SECTORS - 1)
-        if target < count * SECTORS:
-            outward.append((device, target))
-    axes = ("rad", "azi")
-    low = lax.ppermute(up, axes, outward)
-    high = lax.ppermute(down, axes, [(target, device) for device, target in outward])
-    solved = solve(place, source, low, high, *inverse)
+    source, cross, chip = make_source(place, received, *forward)
+    swaps = []
+    for device in range(1, (count - 1) * SECTORS, 2):
+        swaps += [(device, device + SECTORS - 1), (device + SECTORS - 1, device)]
+    cross = lax.ppermute(cross, ("rad", "azi"), swaps)
+    chip = lax.ppermute(chip, "azi", [(i, i ^ 1) for i in range(SECTORS)])
+    solved = solve(place, source, cross, chip, *inverse)
     received = lax.all_to_all(solved.reshape(SECTORS, RANK, LANES), "azi", 0, 0)
     return expand(received, stretch)
 

time: 53.8 us -> 49.8 us (0.926)
  the two profiles are of different devices: /device:TPU:240 before, /device:TPU:256 now
where the time goes in v3:
time: 49.8 us; the launch traced here: 49.5 us
  waiting for transfers between devices  15.5 us (31%)
  blocking collectives  13.1 us (26%)
  starting transfers between devices  12.1 us (24%)
  Pallas kernels  8.64 us (17%)
    all_to_all x1, blocking collectives, per_device(): received = lax.all_to_all(solved.reshape(SECTORS, RANK, LANES), 'azi', 0, 0)  13.1 us
    all_to_all x1, waiting for transfers between devices, per_device(): received = lax.all_to_all(outgoing, 'azi', 0, 0)  11.5 us
    all_to_all x1, starting transfers between devices, per_device(): received = lax.all_to_all(outgoing, 'azi', 0, 0)  5.56 us
    ppermute x1, waiting for transfers between devices, per_device(): cross = lax.ppermute(cross, ('rad', 'azi'), swaps)  3.97 us
    pallas_call x1, Pallas kernels, compress(): call(compress_kernel, [(SECTORS, 3 * HALF, LANES)], [HBM, HBM], [pltpu.VM...  3.59 us
    ppermute x1, starting transfers between devices, per_device(): cross = lax.ppermute(cross, ('rad', 'azi'), swaps)  3.3 us
    ppermute x1, starting transfers between devices, per_device(): chip = lax.ppermute(chip, 'azi', [(i, i ^ 1) for i in range(SECTORS)])  3.22 us
    pallas_call x1, Pallas kernels, solve(): call(solve_kernel, [(SECTORS * RANK, LANES)], [SMEM] + [VMEM] * 5, [pltpu...  2.3 us
  transfers between devices with their start and end apart: 3, of which 2 were waited for; matrix products, arithmetic and copies ran while one was open for 0% of the time, Pallas kernels for 0%

profile of v3, /device:TPU:256, one launch (start us, length us, event | category | flops | bytes accessed | tf_op | source)
XLA Modules:
  0.0 49.5 jit_solution(6971165586571267684)
XLA Ops:
  0.0 0.0 copy-start.1
  0.0 3.6 %compress.1 = f32[16,72,128]{2,1,0:T(8,128)} custom-call(f32[16,128,128]{2,1,0:T(8,128)} %x_hbm.1, bf16[96,256]{1,0:T(8,128)(2,1)} %constant.31.clone.squeeze_hbm), custom_call_target="tpu_custom_call" | custom-call | tf_op jit(solution)/shard_map/compress/pallas_call | solution.py:369
  3.6 0.0 copy-start
  3.6 5.6 %all-to-all-start = ((f32[16,72,128]{2,1,0:T(8,128)}), f32[16,72,128]{2,1,0:T(8,128)S(1)}, u32[]{:S(2)}, u32[]{:S(2)}) async-start(f32[16,72,128]{2,1,0:T(8,128)} %compress.1), calls=%async_computation | async-start | bytes 1179648 | tf_op jit(solution)/shard_map/all_to_all | solution.py:445
  9.2 0.1 pad_add_fusion.place_ref
  9.3 0.0 copy-start.2
  9.3 11.5 %all-to-all-done.p_ref = f32[16,72,128]{2,1,0:T(8,128)S(1)} async-done(((f32[16,72,128]{2,1,0:T(8,128)}), f32[16,72,128]{2,1,0:T(8,128)S(1)}, u32[]{:S(2)}, u32[]{:S(2)}) %all-to-all-start) | async-done | bytes 589856 | tf_op jit(solution)/shard_map/all_to_all | solution.py:445
  20.8 0.0 copy-done.1
  20.8 0.0 copy-done
  20.8 0.0 copy-start.3
  20.8 1.3 %make_source.1 = (f32[192,512]{1,0:T(8,128)S(1)}, f32[56,512]{1,0:T(8,128)S(1)}, f32[56,512]{1,0:T(8,128)S(1)}) custom-call(s32[4]{0:T(128)S(1)} %pad_add_fusion.place_ref, f32[16,72,128]{2,1,0:T(8,128)S(1)} %all-to-all-done.p_ref, bf16[768,512]{1,0:T(8,128)(2,1)S(1)} %copy-done.1, bf16[768,512]{1,0:T(8,128)(2,1)S(1)} %copy-done), custom_call_target="tpu_custom_call" | custom-call | tf_op jit(solution)/shard_map/make_source/pallas_call | solution.py:386
  22.1 3.3 %collective-permute-start = (f32[56,512]{1,0:T(8,128)S(1)}, f32[56,512]{1,0:T(8,128)S(1)}, u32[]{:S(2)}, u32[]{:S(2)}) collective-permute-start(f32[56,512]{1,0:T(8,128)S(1)} %get-tuple-element.9), channel_id=1, source_target_pairs={{1,16},{16,1},{3,18},{18,3},{5,20},{20,5},{7,22},{22,7},{9,24},{24... | collective-permute-start | bytes 344072 | tf_op jit(solution)/shard_map/ppermute | solution.py:450
  25.4 3.2 %collective-permute-start.1 = (f32[56,512]{1,0:T(8,128)S(1)}, f32[56,512]{1,0:T(8,128)S(1)}, u32[]{:S(2)}, u32[]{:S(2)}) collective-permute-start(f32[56,512]{1,0:T(8,128)S(1)} %get-tuple-element.10), channel_id=1, source_target_pairs={{0,1},{1,0},{2,3},{3,2},{4,5},{5,4},{6,7},{7,6},{8,9},{9,8},{10,11... | collective-permute-start | bytes 344072 | tf_op jit(solution)/shard_map/ppermute | solution.py:451
  28.6 4.0 %collective-permute-done.cross_ref = f32[56,512]{1,0:T(8,128)S(1)} collective-permute-done((f32[56,512]{1,0:T(8,128)S(1)}, f32[56,512]{1,0:T(8,128)S(1)}, u32[]{:S(2)}, u32[]{:S(2)}) %collective-permute-start) | collective-permute-done | bytes 114720 | tf_op jit(solution)/shard_map/ppermute | solution.py:450
  32.6 0.0 collective-permute-done.1.chip_ref
  32.6 0.0 copy-done.2
  32.6 0.0 copy-done.3
  32.6 2.3 %solve.1 = f32[768,128]{1,0:T(8,128)S(1)} custom-call(s32[4]{0:T(128)S(1)} %pad_add_fusion.place_ref, f32[192,512]{1,0:T(8,128)S(1)} %get-tuple-element.8.s_ref, f32[56,512]{1,0:T(8,128)S(1)} %collective-permute-done.cross_ref, f32[56,512]{1,0:T(8,128)S(1)} %collective-permute-done.1.chip_ref, bf16[768,512]{1,0:T(8,128)(2,1)S(1)} %copy-done.3, ...), custom_call_target="tpu_custom_call" | custom-call | tf_op jit(solution)/shard_map/solve/pallas_call | solution.py:397
  34.9 0.0 copy-start.4
  34.9 13.1 %all_to_all.10.q_ref = f32[16,48,128]{2,1,0:T(8,128)S(1)} all-to-all(f32[16,48,128]{2,1,0:T(8,128)S(1)} %bitcast.4), channel_id=1, replica_groups=mesh['rad'=32,'azi'=16] {'azi'}, dimensions={0} | all-to-all | bytes 786432 | tf_op jit(solution)/shard_map/all_to_all | solution.py:453
  48.0 0.0 copy-done.4
  48.0 1.5 %expand.1 = f32[16,128,128]{2,1,0:T(8,128)} custom-call(f32[16,48,128]{2,1,0:T(8,128)S(1)} %all_to_all.10.q_ref, bf16[128,192]{1,0:T(8,128)(2,1)S(1)} %copy-done.4), custom_call_target="tpu_custom_call" | custom-call | tf_op jit(solution)/shard_map/expand/pallas_call | solution.py:414
Async XLA Ops:
  0.0 20.8 %copy-start.1 = (bf16[768,512]{1,0:T(8,128)(2,1)S(1)}, bf16[768,512]{1,0:T(8,128)(2,1)}, u32[]{:S(2)}) copy-start(bf16[768,512]{1,0:T(8,128)(2,1)} %constant.32.clone.high_ref) | copy-start | bytes 2359300
  3.6 17.2 %copy-start = (bf16[768,512]{1,0:T(8,128)(2,1)S(1)}, bf16[768,512]{1,0:T(8,128)(2,1)}, u32[]{:S(2)}) copy-start(bf16[768,512]{1,0:T(8,128)(2,1)} %constant.33.clone.low_ref) | copy-start | bytes 2359300
  3.6 17.2 %all-to-all-start = ((f32[16,72,128]{2,1,0:T(8,128)}), f32[16,72,128]{2,1,0:T(8,128)S(1)}, u32[]{:S(2)}, u32[]{:S(2)}) async-start(f32[16,72,128]{2,1,0:T(8,128)} %compress.1), calls=%async_computation | async-start | bytes 1179648 | tf_op jit(solution)/shard_map/all_to_all | solution.py:445
  9.3 23.3 %copy-start.2 = (bf16[768,512]{1,0:T(8,128)(2,1)S(1)}, bf16[768,512]{1,0:T(8,128)(2,1)}, u32[]{:S(2)}) copy-start(bf16[768,512]{1,0:T(8,128)(2,1)} %constant.35.clone.vl_ref) | copy-start | bytes 2359300
  20.8 11.8 %copy-start.3 = (bf16[768,512]{1,0:T(8,128)(2,1)S(1)}, bf16[768,512]{1,0:T(8,128)(2,1)}, u32[]{:S(2)}) copy-start(bf16[768,512]{1,0:T(8,128)(2,1)} %constant.34.clone.vh_ref) | copy-start | bytes 2359300
  22.1 10.5 %collective-permute-start = (f32[56,512]{1,0:T(8,128)S(1)}, f32[56,512]{1,0:T(8,128)S(1)}, u32[]{:S(2)}, u32[]{:S(2)}) collective-permute-start(f32[56,512]{1,0:T(8,128)S(1)} %get-tuple-element.9), channel_id=1, source_target_pairs={{1,16},{16,1},{3,18},{18,3},{5,20},{20,5},{7,22},{22,7},{9,24},{24... | collective-permute-start | bytes 344072 | tf_op jit(solution)/shard_map/ppermute | solution.py:450
  25.4 7.2 %collective-permute-start.1 = (f32[56,512]{1,0:T(8,128)S(1)}, f32[56,512]{1,0:T(8,128)S(1)}, u32[]{:S(2)}, u32[]{:S(2)}) collective-permute-start(f32[56,512]{1,0:T(8,128)S(1)} %get-tuple-element.10), channel_id=1, source_target_pairs={{0,1},{1,0},{2,3},{3,2},{4,5},{5,4},{6,7},{7,6},{8,9},{9,8},{10,11... | collective-permute-start | bytes 344072 | tf_op jit(solution)/shard_map/ppermute | solution.py:451
  34.9 13.1 %copy-start.4 = (bf16[128,192]{1,0:T(8,128)(2,1)S(1)}, bf16[128,192]{1,0:T(8,128)(2,1)}, u32[]{:S(2)}) copy-start(bf16[128,192]{1,0:T(8,128)(2,1)} %constant.36.clone.stretch_ref) | copy-start | bytes 147460

commit v4 on v2

v4 whole, which is shorter than its diff:
```python
import functools
import math

import jax
import jax.numpy as jnp
import numpy as np
from jax import lax
from jax.experimental import pallas as pl
from jax.experimental.pallas import tpu as pltpu
from jax.sharding import PartitionSpec as P

NPHI = 2048
MODES = 256
SWEEPS = 4
SECTORS = 16
SECTOR = NPHI // SECTORS
COEFS = 2 * MODES
RANK = 48
ROWS = 16
DEPTH = 128
GROUP = 8
LANES = 128
HALF = RANK // 2
BLOCKS = 8
BLOCK_ROWS = 8
EXTENDED = BLOCK_ROWS + 6
CELLS = 3 * GROUP * BLOCK_ROWS
CHUNKS = 4

low_bound = 0.1
high_bound = 2.0
theta = 0.5 * (high_bound + low_bound)
delta = 0.5 * (high_bound - low_bound)
sigma = theta / delta
four_pi = 4.0 * math.pi

BF = jnp.bfloat16
F32 = jnp.float32


def split_table(table):
    high = table.astype(np.float32).astype(BF)
    low = (table - high.astype(np.float64)).astype(np.float32).astype(BF)
    return high, low


@functools.cache
def tables():
    modes = np.arange(MODES)
    angle = 2.0 * np.pi * ((np.arange(SECTOR)[:, None] * modes[None, :]) % NPHI) / NPHI
    first = np.concatenate([np.cos(angle), np.sin(angle)], axis=1)
    left, _, _ = np.linalg.svd(first, full_matrices=False)
    left = left[:, :RANK]
    cores = []
    for sector in range(SECTORS):
        cells = sector * SECTOR + np.arange(SECTOR)
        angle = 2.0 * np.pi * ((cells[:, None] * modes[None, :]) % NPHI) / NPHI
        cores.append(left.T @ np.concatenate([np.cos(angle), np.sin(angle)], axis=1))
    core = np.concatenate(cores, axis=0)
    weight = np.where(np.tile(modes, 2) == 0, 1.0, 2.0)
    left_high, left_low = split_table(left)
    ordered = core.reshape(SECTORS, 2, HALF, COEFS).transpose(1, 0, 2, 3)
    forward = split_table(ordered.reshape(SECTORS * RANK, COEFS) * (-four_pi / NPHI))
    inverse = split_table(core * weight[None, :])
    squeeze = np.concatenate(
        [
            np.concatenate([left_high.T, left_high.T], axis=1),
            np.concatenate([left_low.T, left_low.T], axis=1),
        ],
        axis=0,
    )
    stretch = np.concatenate([left_high, left_high, left_low, left_low], axis=1)
    return squeeze, forward, inverse, stretch


def halves(value):
    high = value.astype(BF)
    low = (value - high.astype(F32)).astype(BF)
    return high, low


def dot(a, b):
    return jnp.dot(a, b, preferred_element_type=F32)


def swap_groups(blocks, size, bits):
    group = lax.broadcasted_iota(jnp.int32, next(iter(blocks.values())).shape, 1) // size
    for bit in bits:
        keep = (group & bit) == 0
        for i in list(blocks):
            if i & bit:
                continue
            j = i | bit
            one, two = blocks[i], blocks[j]
            blocks[i] = jnp.where(keep, one, pltpu.roll(two, size * bit, 1))
            blocks[j] = jnp.where(keep, pltpu.roll(one, LANES - size * bit, 1), two)
    return blocks


def compress_kernel(high_ref, low_ref, squeeze_ref, out_ref, y_ref):
    squeeze = squeeze_ref[...]
    for r in range(0, ROWS, 2):
        rows = slice(r, r + 2)
        pair = [jnp.concatenate([h, l], axis=0) for h, l in zip(high_ref[rows], low_ref[rows])]
        y = dot(squeeze, jnp.concatenate(pair, axis=1))
        y = y[:RANK] + y[RANK:]
        y_ref[r] = y[:, :LANES]
        y_ref[r + 1] = y[:, LANES:]
    for side in range(2):
        first = side * BLOCK_ROWS
        for c in range(0, HALF, 8):
            blocks = {}
            for r in range(BLOCK_ROWS):
                for half in range(2):
                    start = half * HALF + c
                    blocks[half * BLOCK_ROWS + r] = y_ref[first + r, start : start + 8, :]
            swap_groups(blocks, GROUP, (1, 2, 4, 8))
            for g in blocks:
                for j in range(g % 2, 3, 2):
                    at = j * HALF + c
                    out_ref[(g - j) % SECTORS + side, at : at + 8, :] = blocks[g]


def source_kernel(p_ref, high_ref, low_ref, s_ref, cross_ref, chip_ref):
    turned = []
    for j in range(3):
        block = p_ref[:, j * HALF : (j + 1) * HALF, :].reshape(SECTORS * HALF, LANES).T
        turned.append(jnp.concatenate([block[:64], block[64:]], axis=1))
    cells_high, cells_low = halves(jnp.concatenate(turned, axis=0))
    both = jnp.concatenate([cells_high, cells_low], axis=0)
    for n in range(0, COEFS, 256):
        wide = dot(both, high_ref[:, n : n + 256])
        s_ref[:, n : n + 256] = (
            wide[:CELLS] + wide[CELLS:] + dot(cells_high, low_ref[:, n : n + 256])
        )
    level = lax.broadcasted_iota(jnp.int32, (8, COEFS), 0)

    def at(j, r):
        return s_ref[pl.ds(pl.multiple_of(j * 64 + r * 8, 8), 8), :]

    def pack(ref, near, middle, far):
        ref[0:8, :] = jnp.where(level < 4, at(2, far), at(0, far))
        ref[8:16, :] = jnp.where(level < 2, pltpu.roll(at(2, middle), 5, 0), at(0, near))
        ref[16:24, :] = at(2, near)
        ref[24:32, :] = jnp.where(level < 3, at(2, middle), at(0, middle))
        ref[32:40, :] = at(1, near)
        ref[40:48, :] = at(1, middle)
        ref[48:56, :] = at(1, far)

    core = lax.axis_index("azi") & 1
    start, back = core * 7, 1 - 2 * core
    pack(cross_ref, start, start + back, start + 2 * back)
    start, back = 7 - start, -back
    pack(chip_ref, start, start + back, start + 2 * back)


def unpack(load, distance, level):
    if distance == 3:
        both = load(0)
        return [both, load(48), both]
    if distance == 2:
        both = load(24)
        rest = pltpu.roll(load(8), 3, 0)
        return [both, load(40), jnp.where(level < 3, both, rest)]
    return [load(8), load(32), load(16)]


def factors():
    steps = []
    ratio = 1.0 / sigma
    for _ in range(SWEEPS - 1):
        following = 1.0 / (2.0 * sigma - ratio)
        steps.append((following * ratio, 2.0 * following / delta))
        ratio = following
    return steps


def vertical(center, level, cut):
    above = [pltpu.roll(x, 7, 0) for x in center]
    below = [pltpu.roll(x, 1, 0) for x in center]
    return [
        jnp.where(level == 7, above[1], above[0]) + below[0],
        jnp.where(level == 7, above[2] * cut, above[1])
        + jnp.where(level == 0, below[0], below[1]),
        above[2] + jnp.where(level == 0, below[1] * cut, below[2]),
    ]


def window_cut():
    last = (lax.axis_index("azi") >> 1) == BLOCKS - 1
    return jnp.where(jnp.full((8, LANES), last), 0.0, 1.0).astype(F32)


def main_kernel(count, s_ref, own_ref, inverse_ref, weight_ref):
    shape = (8, LANES)
    level = lax.broadcasted_iota(jnp.int32, shape, 0)
    lane = lax.broadcasted_iota(jnp.int32, shape, 1)
    core = lax.axis_index("azi") & 1
    row_first = lax.axis_index("rad") * ROWS + core * BLOCK_ROWS
    cut = window_cut()

    for e in range(EXTENDED):
        row = jnp.full(shape, row_first + (e - 3), jnp.int32)
        inverse = 1.0 / (row.astype(F32) + 0.5)
        weight_ref[e, 0] = 1.0 + 0.5 * inverse
        weight_ref[e, 1] = 1.0 - 0.5 * inverse
        good = jnp.where((row >= 0) & (row < count * ROWS), 1.0, 0.0).astype(F32)
        for t in range(2):
            ratio = (lane + t * LANES).astype(F32) * inverse
            inverse_ref[t, e] = good / (4.0 + ratio * ratio)

    ratios = factors()

    @pl.loop(0, 4)
    def _(tile):
        lanes = pl.ds(pl.multiple_of(tile * LANES, LANES), LANES)
        table = tile % 2
        given, scale, step = {}, {}, {}
        state = [{} for _ in range(SWEEPS)]
        for newest in range(3, EXTENDED + SWEEPS - 1):
            e = newest
            if e < 11:
                starts = [j * 64 + (e - 3) * 8 for j in range(3)]
                given[e] = [s_ref[start : start + 8, lanes] for start in starts]
                scale[e] = inverse_ref[table, e]
                step[e] = [g * scale[e] * (1.0 / theta) for g in given[e]]
                state[0][e] = step[e]
            for sweep in range(1, SWEEPS):
                e = newest - sweep
                reach = min(sweep, SWEEPS - 1 - sweep)
                if not 3 - reach <= e < 11 + reach:
                    continue
                keep, push = ratios[sweep - 1]
                steps, values = advance(
                    keep,
                    push,
                    state[sweep - 1],
                    given.get(e),
                    step.get(e),
                    e,
                    inverse_ref[table, e],
                    weight_ref[e, 0],
                    weight_ref[e, 1],
                    level,
                    cut,
                )
                step[e] = steps
                state[sweep][e] = values
            e = newest - (SWEEPS - 1)
            if 3 <= e < 11:
                x = state[SWEEPS - 1][e]
                at = (e - 3) * 16
                own_ref[at : at + 8, lanes] = jnp.where(level < 4, x[2], x[0])
                own_ref[at + 8 : at + 16, lanes] = x[1]


def advance(keep, push, old, given, step, e, scale, plus, minus, level, cut):
    center = old.get(e)
    near = vertical(center, level, cut) if center is not None else None
    steps, values = [], []
    for j in range(3):
        terms = []
        if given is not None:
            terms.append(given[j])
        if near is not None:
            terms.append(near[j])
        if e + 1 in old:
            terms.append(plus * old[e + 1][j])
        if e - 1 in old:
            terms.append(minus * old[e - 1][j])
        move = (push * scale) * sum(terms[1:], terms[0])
        if center is not None:
            move = move - push * center[j]
        if step is not None:
            move = move + keep * step[j]
        steps.append(move)
        values.append(move if center is None else center[j] + move)
    return steps, values


def edge_kernel(
    main_ref, inverse_ref, weight_ref, cross_ref, chip_ref, vh_ref, vl_ref, out_ref, own_ref
):
    level = lax.broadcasted_iota(jnp.int32, (8, LANES), 0)
    core = lax.axis_index("azi") & 1
    cut = window_cut()
    ratios = factors()
    own_ref[...] = main_ref[...]

    @pl.loop(0, 4)
    def _(tile):
        lanes = pl.ds(pl.multiple_of(tile * LANES, LANES), LANES)
        table = tile % 2
        for ref, turned in ((cross_ref, core), (chip_ref, 1 - core)):
            at = [t + turned * (EXTENDED - 1 - 2 * t) for t in range(6)]
            given = {
                t: unpack(lambda start: ref[start : start + 8, lanes], 3 - t, level)
                for t in range(3)
            }
            scale = [inverse_ref[table, e] for e in at]
            step = {t: [g * scale[t] * (1.0 / theta) for g in given[t]] for t in given}
            state = dict(step)
            for sweep in range(1, SWEEPS):
                keep, push = ratios[sweep - 1]
                fresh = {}
                for t in range(sweep, sweep + 3):
                    steps, fresh[t] = advance(
                        keep,
                        push,
                        state,
                        given.get(t),
                        step.get(t),
                        t,
                        scale[t],
                        weight_ref[at[t], turned],
                        weight_ref[at[t], 1 - turned],
                        level,
                        cut,
                    )
                    step[t] = steps
                state = fresh
            for t in range(3, 6):
                x = state[t]
                start = pl.multiple_of((at[t] - 3) * 16, 16)
                own_ref[pl.ds(start, 8), lanes] += jnp.where(level < 4, x[2], x[0])
                own_ref[pl.ds(start + 8, 8), lanes] += x[1]

    own_high, own_low = halves(own_ref[...])
    both = jnp.concatenate([own_high, own_low], axis=0)

    def across(a, b):
        return lax.dot_general(a, b, (((1,), (1,)), ((), ())), preferred_element_type=F32)

    step_rows = 192
    for m in range(0, SECTORS * RANK, step_rows):
        wide = across(vh_ref[m : m + step_rows, :], both)
        out_ref[m : m + step_rows, :] = (
            wide[:, :LANES]
            + wide[:, LANES:]
            + across(vl_ref[m : m + step_rows, :], own_high)
        )


def expand_kernel(q_ref, stretch_ref, out_hbm, y_ref, out_ref, sems):
    stretch = stretch_ref[...]
    first = lax.broadcasted_iota(jnp.int32, (8, LANES), 1) % (2 * GROUP) < 4
    rows = ROWS // CHUNKS
    copies = []
    for side in range(2):
        for c in range(0, RANK, 8):
            held = [q_ref[2 * b + side, c : c + 8, :] for b in range(BLOCKS)]
            blocks = {b: jnp.where(first, held[b - 1], held[b]) for b in range(BLOCKS)}
            swap_groups(blocks, 2 * GROUP, (1, 2, 4))
            for r in range(BLOCK_ROWS):
                y_ref[side * BLOCK_ROWS + r, c : c + 8, :] = blocks[r]
        for r in range(side * BLOCK_ROWS, (side + 1) * BLOCK_ROWS, 2):
            columns = []
            for k in range(2):
                high, low = halves(y_ref[r + k])
                columns.append(jnp.concatenate([high, low, high, low], axis=0))
            wide = dot(stretch, jnp.concatenate(columns, axis=1))
            out_ref[r] = wide[:, :LANES]
            out_ref[r + 1] = wide[:, LANES:]
            if (r + 2) % rows == 0:
                part = pl.ds(r + 2 - rows, rows)
                sem = sems.at[len(copies)]
                copies.append(pltpu.make_async_copy(out_ref.at[part], out_hbm.at[part], sem))
                copies[-1].start()
    for copy in copies:
        copy.wait()


VMEM = pl.BlockSpec(memory_space=pltpu.VMEM)
HBM = pl.BlockSpec(memory_space=pltpu.HBM)


def call(kernel, outs, in_specs, scratch, name, out_space=VMEM, **options):
    single = len(outs) == 1
    shapes = [jax.ShapeDtypeStruct(shape, F32) for shape in outs]
    return pl.pallas_call(
        kernel,
        out_shape=shapes[0] if single else shapes,
        in_specs=in_specs,
        out_specs=out_space if single else [out_space] * len(outs),
        scratch_shapes=scratch,
        compiler_params=pltpu.CompilerParams(vmem_limit_bytes=40 * 1024 * 1024),
        name=name,
        **options,
    )


def compress(high, low, squeeze, **options):
    return call(
        compress_kernel,
        [(SECTORS, 3 * HALF, LANES)],
        [VMEM] * 3,
        [pltpu.VMEM((ROWS, RANK, LANES), F32)],
        "compress",
        **options,
    )(high, low, squeeze)


def make_source(received, high, low, **options):
    return call(
        source_kernel,
        [(CELLS, COEFS), (56, COEFS), (56, COEFS)],
        [VMEM] * 3,
        [],
        "make_source",
        **options,
    )(received, high, low)


def solve_main(count, source, **options):
    return call(
        functools.partial(main_kernel, count),
        [(LANES, COEFS), (2, EXTENDED, 8, LANES), (EXTENDED, 2, 8, LANES)],
        [VMEM],
        [],
        "solve_main",
        cost_estimate=pl.CostEstimate(
            flops=40_000_000, bytes_accessed=1_000_000, transcendentals=0
        ),
        **options,
    )(source)


def solve_edge(main, inverse, weight, cross, chip, v_high, v_low, **options):
    return call(
        edge_kernel,
        [(SECTORS * RANK, LANES)],
        [VMEM] * 7,
        [pltpu.VMEM((LANES, COEFS), F32)],
        "solve_edge",
        **options,
    )(main, inverse, weight, cross, chip, v_high, v_low)


def expand(received, stretch, **options):
    return call(
        expand_kernel,
        [(ROWS, SECTOR, DEPTH)],
        [VMEM] * 2,
        [
            pltpu.VMEM((ROWS, RANK, LANES), F32),
            pltpu.VMEM((ROWS, SECTOR, DEPTH), F32),
            pltpu.SemaphoreType.DMA((CHUNKS,)),
        ],
        "expand",
        out_space=HBM,
        **options,
    )(received, stretch)


def split_rows(density):
    high = lax.reduce_precision(density, 8, 7)
    return high.astype(BF), (density - high).astype(BF)


def per_device(density):
    squeeze, forward, inverse, stretch = (
        jax.tree.map(jnp.asarray, item) for item in tables()
    )
    count = lax.axis_size("rad")
    outgoing = compress(*split_rows(density), squeeze)
    received = lax.all_to_all(outgoing, "azi", 0, 0)
    source, cross, chip = make_source(received, *forward)
    swaps = []
    for device in range(1, (count - 1) * SECTORS, 2):
        swaps += [(device, device + SECTORS - 1), (device + SECTORS - 1, device)]
    cross = lax.ppermute(cross, ("rad", "azi"), swaps)
    chip = lax.ppermute(chip, "azi", [(i, i ^ 1) for i in range(SECTORS)])
    main, scales, weights = solve_main(count, source)
    solved = solve_edge(main, scales, weights, cross, chip, *inverse)
    received = lax.all_to_all(solved.reshape(SECTORS, RANK, LANES), "azi", 0, 0)
    return expand(received, stretch)


def solution(mesh):
    spec = P("rad", "azi", None)
    return jax.shard_map(
        per_device, mesh=mesh, in_specs=(spec,), out_specs=spec, check_vma=False
    )
```

time: 53.8 us -> 46.5 us (0.86)
  the two profiles are of different devices: /device:TPU:240 before, /device:TPU:256 now
where the time goes in v4:
time: 46.5 us; the launch traced here: 46.3 us
  blocking collectives  30 us (65%)
  starting transfers between devices  6.52 us (14%)
  Pallas kernels  4.96 us (11%)
  waiting for transfers between devices  3.14 us (7%)
  other arithmetic  1.49 us (3%)
    all_to_all x1, blocking collectives, per_device(): received = lax.all_to_all(outgoing, 'azi', 0, 0)  16.9 us
    all_to_all x1, blocking collectives, per_device(): received = lax.all_to_all(solved.reshape(SECTORS, RANK, LANES), 'azi', 0, 0)  13.1 us
    ppermute x1, starting transfers between devices, per_device(): cross = lax.ppermute(cross, ('rad', 'azi'), swaps)  4.03 us
    ppermute x1, waiting for transfers between devices, per_device(): cross = lax.ppermute(cross, ('rad', 'azi'), swaps)  3.14 us
    ppermute x1, starting transfers between devices, per_device(): chip = lax.ppermute(chip, 'azi', [(i, i ^ 1) for i in range(SECTORS)])  2.49 us
    convert_element_type x1, other arithmetic, split_rows(): return (high.astype(BF), (density - high).astype(BF))  1.49 us
    pallas_call x1, Pallas kernels, expand(): call(expand_kernel, [(ROWS, SECTOR, DEPTH)], [VMEM] * 2, [pltpu.VMEM((ROW...  1.46 us
    pallas_call x1, Pallas kernels, solve_edge(): call(edge_kernel, [(SECTORS * RANK, LANES)], [VMEM] * 7, [pltpu.VMEM((LAN...  1.1 us
  transfers between devices with their start and end apart: 2, of which 1 were waited for; matrix products, arithmetic and copies ran while one was open for 0% of the time, Pallas kernels for 2%

profile of v4, /device:TPU:256, one launch (start us, length us, event | category | flops | bytes accessed | tf_op | source)
XLA Modules:
  0.0 46.3 jit_solution(7282226395526106710)
XLA Ops:
  0.0 0.0 copy-start.5
  0.0 1.5 %fusion = (bf16[16,128,128]{2,1,0:T(8,128)(2,1)S(1)}, bf16[16,128,128]{2,1,0:T(8,128)(2,1)S(1)}) fusion(f32[16,128,128]{2,1,0:T(8,128)} %param.7), kind=kLoop, calls=%fused_computation.2 | loop fusion | flops 1048576 | bytes 2097152 | tf_op jit(solution)/shard_map/convert_element_type | solution.py:457
  1.5 0.0 copy-done.5
  1.5 0.0 copy-start.1
  1.5 0.7 %compress.1 = f32[16,72,128]{2,1,0:T(8,128)S(1)} custom-call(bf16[16,128,128]{2,1,0:T(8,128)(2,1)S(1)} %get-tuple-element.18.high_ref, bf16[16,128,128]{2,1,0:T(8,128)(2,1)S(1)} %get-tuple-element.17.low_ref, bf16[96,256]{1,0:T(8,128)(2,1)S(1)} %copy-done.5), custom_call_target="tpu_custom_call" | custom-call | tf_op jit(solution)/shard_map/compress/pallas_call | solution.py:393
  2.2 0.0 copy-start
  2.2 16.9 %all_to_all.10.p_ref = f32[16,72,128]{2,1,0:T(8,128)S(1)} all-to-all(f32[16,72,128]{2,1,0:T(8,128)S(1)} %compress.1), channel_id=1, replica_groups=mesh['rad'=32,'azi'=16] {'azi'}, dimensions={0} | all-to-all | bytes 1179648 | tf_op jit(solution)/shard_map/all_to_all | solution.py:466
  19.2 0.0 copy-done.1
  19.2 0.0 copy-done
  19.2 0.0 copy-start.2
  19.2 0.0 copy-start.3
  19.2 0.8 %make_source.1 = (f32[192,512]{1,0:T(8,128)S(1)}, f32[56,512]{1,0:T(8,128)S(1)}, f32[56,512]{1,0:T(8,128)S(1)}) custom-call(f32[16,72,128]{2,1,0:T(8,128)S(1)} %all_to_all.10.p_ref, bf16[768,512]{1,0:T(8,128)(2,1)S(1)} %copy-done.1, bf16[768,512]{1,0:T(8,128)(2,1)S(1)} %copy-done), custom_call_target="tpu_custom_call" | custom-call | tf_op jit(solution)/shard_map/make_source/pallas_call | solution.py:404
  20.0 4.0 %collective-permute-start = (f32[56,512]{1,0:T(8,128)S(1)}, f32[56,512]{1,0:T(8,128)S(1)}, u32[]{:S(2)}, u32[]{:S(2)}) collective-permute-start(f32[56,512]{1,0:T(8,128)S(1)} %get-tuple-element.15), channel_id=1, source_target_pairs={{1,16},{16,1},{3,18},{18,3},{5,20},{20,5},{7,22},{22,7},{9,24},{24... | collective-permute-start | bytes 344072 | tf_op jit(solution)/shard_map/ppermute | solution.py:471
  24.0 2.5 %collective-permute-start.1 = (f32[56,512]{1,0:T(8,128)S(1)}, f32[56,512]{1,0:T(8,128)S(1)}, u32[]{:S(2)}, u32[]{:S(2)}) collective-permute-start(f32[56,512]{1,0:T(8,128)S(1)} %get-tuple-element.16), channel_id=1, source_target_pairs={{0,1},{1,0},{2,3},{3,2},{4,5},{5,4},{6,7},{7,6},{8,9},{9,8},{10,11... | collective-permute-start | bytes 344072 | tf_op jit(solution)/shard_map/ppermute | solution.py:472
  26.5 0.9 %solve_main.1 = (f32[128,512]{1,0:T(8,128)S(1)}, f32[2,14,8,128]{3,2,1,0:T(8,128)S(1)}, f32[14,2,8,128]{3,2,1,0:T(8,128)S(1)}) custom-call(f32[192,512]{1,0:T(8,128)S(1)} %get-tuple-element.11.s_ref), custom_call_target="tpu_custom_call" | custom-call | flops 40000000 | bytes 1000000 | tf_op jit(solution)/shard_map/solve_main/pallas_call | solution.py:415
  27.4 3.1 %collective-permute-done.cross_ref = f32[56,512]{1,0:T(8,128)S(1)} collective-permute-done((f32[56,512]{1,0:T(8,128)S(1)}, f32[56,512]{1,0:T(8,128)S(1)}, u32[]{:S(2)}, u32[]{:S(2)}) %collective-permute-start) | collective-permute-done | bytes 114720 | tf_op jit(solution)/shard_map/ppermute | solution.py:471
  30.6 0.0 collective-permute-done.1.chip_ref
  30.6 0.0 copy-done.2
  30.6 0.0 copy-done.3
  30.6 1.1 %solve_edge.1 = f32[768,128]{1,0:T(8,128)S(1)} custom-call(f32[128,512]{1,0:T(8,128)S(1)} %get-tuple-element.12.main_ref, f32[2,14,8,128]{3,2,1,0:T(8,128)S(1)} %get-tuple-element.13.inverse_ref, f32[14,2,8,128]{3,2,1,0:T(8,128)S(1)} %get-tuple-element.14.weight_ref, f32[56,512]{1,0:T(8,128)S(1)} %collective-permute-done.cross_ref, ...), custom_call_target="tpu_custom_call" | custom-call | tf_op jit(solution)/shard_map/solve_edge/pallas_call | solution.py:429
  31.7 0.0 copy-start.4
  31.7 13.1 %all_to_all.11.q_ref = f32[16,48,128]{2,1,0:T(8,128)S(1)} all-to-all(f32[16,48,128]{2,1,0:T(8,128)S(1)} %bitcast.1), channel_id=1, replica_groups=mesh['rad'=32,'azi'=16] {'azi'}, dimensions={0} | all-to-all | bytes 786432 | tf_op jit(solution)/shard_map/all_to_all | solution.py:475
  44.8 0.0 copy-done.4
  44.8 1.5 %expand.1 = f32[16,128,128]{2,1,0:T(8,128)} custom-call(f32[16,48,128]{2,1,0:T(8,128)S(1)} %all_to_all.11.q_ref, bf16[128,192]{1,0:T(8,128)(2,1)S(1)} %copy-done.4), custom_call_target="tpu_custom_call" | custom-call | tf_op jit(solution)/shard_map/expand/pallas_call | solution.py:440
Async XLA Ops:
  0.0 1.5 %copy-start.5 = (bf16[96,256]{1,0:T(8,128)(2,1)S(1)}, bf16[96,256]{1,0:T(8,128)(2,1)}, u32[]{:S(2)}) copy-start(bf16[96,256]{1,0:T(8,128)(2,1)} %constant.12.clone.squeeze_ref) | copy-start | bytes 147460
  1.5 17.7 %copy-start.1 = (bf16[768,512]{1,0:T(8,128)(2,1)S(1)}, bf16[768,512]{1,0:T(8,128)(2,1)}, u32[]{:S(2)}) copy-start(bf16[768,512]{1,0:T(8,128)(2,1)} %constant.13.clone.high_ref) | copy-start | bytes 2359300
  2.2 17.0 %copy-start = (bf16[768,512]{1,0:T(8,128)(2,1)S(1)}, bf16[768,512]{1,0:T(8,128)(2,1)}, u32[]{:S(2)}) copy-start(bf16[768,512]{1,0:T(8,128)(2,1)} %constant.14.clone.low_ref) | copy-start | bytes 2359300
  19.2 11.4 %copy-start.2 = (bf16[768,512]{1,0:T(8,128)(2,1)S(1)}, bf16[768,512]{1,0:T(8,128)(2,1)}, u32[]{:S(2)}) copy-start(bf16[768,512]{1,0:T(8,128)(2,1)} %constant.16.clone.vl_ref) | copy-start | bytes 2359300
  19.2 11.4 %copy-start.3 = (bf16[768,512]{1,0:T(8,128)(2,1)S(1)}, bf16[768,512]{1,0:T(8,128)(2,1)}, u32[]{:S(2)}) copy-start(bf16[768,512]{1,0:T(8,128)(2,1)} %constant.15.clone.vh_ref) | copy-start | bytes 2359300
  20.0 10.6 %collective-permute-start = (f32[56,512]{1,0:T(8,128)S(1)}, f32[56,512]{1,0:T(8,128)S(1)}, u32[]{:S(2)}, u32[]{:S(2)}) collective-permute-start(f32[56,512]{1,0:T(8,128)S(1)} %get-tuple-element.15), channel_id=1, source_target_pairs={{1,16},{16,1},{3,18},{18,3},{5,20},{20,5},{7,22},{22,7},{9,24},{24... | collective-permute-start | bytes 344072 | tf_op jit(solution)/shard_map/ppermute | solution.py:471
  24.0 6.6 %collective-permute-start.1 = (f32[56,512]{1,0:T(8,128)S(1)}, f32[56,512]{1,0:T(8,128)S(1)}, u32[]{:S(2)}, u32[]{:S(2)}) collective-permute-start(f32[56,512]{1,0:T(8,128)S(1)} %get-tuple-element.16), channel_id=1, source_target_pairs={{0,1},{1,0},{2,3},{3,2},{4,5},{5,4},{6,7},{7,6},{8,9},{9,8},{10,11... | collective-permute-start | bytes 344072 | tf_op jit(solution)/shard_map/ppermute | solution.py:472
  31.7 13.1 %copy-start.4 = (bf16[128,192]{1,0:T(8,128)(2,1)S(1)}, bf16[128,192]{1,0:T(8,128)(2,1)}, u32[]{:S(2)}) copy-start(bf16[128,192]{1,0:T(8,128)(2,1)} %constant.17.clone.stretch_ref) | copy-start | bytes 147460

commit v5 on v4

--- a/solution.py
+++ b/solution.py
@@ -92,8 +92,13 @@
                 continue
             j = i | bit
             one, two = blocks[i], blocks[j]
-            blocks[i] = jnp.where(keep, one, pltpu.roll(two, size * bit, 1))
-            blocks[j] = jnp.where(keep, pltpu.roll(one, LANES - size * bit, 1), two)
+            if 2 * size * bit == LANES:
+                up = down = pltpu.roll(jnp.where(keep, two, one), LANES // 2, 1)
+            else:
+                up = pltpu.roll(two, size * bit, 1)
+                down = pltpu.roll(one, LANES - size * bit, 1)
+            blocks[i] = jnp.where(keep, one, up)
+            blocks[j] = jnp.where(keep, down, two)
     return blocks
 
 
@@ -287,7 +292,7 @@
     ratios = factors()
     own_ref[...] = main_ref[...]
 
-    @pl.loop(0, 4)
+    @pl.loop(0, 4, unroll=4)
     def _(tile):
         lanes = pl.ds(pl.multiple_of(tile * LANES, LANES), LANES)
         table = tile % 2
@@ -331,7 +336,7 @@
     def across(a, b):
         return lax.dot_general(a, b, (((1,), (1,)), ((), ())), preferred_element_type=F32)
 
-    step_rows = 192
+    step_rows = 384
     for m in range(0, SECTORS * RANK, step_rows):
         wide = across(vh_ref[m : m + step_rows, :], both)
         out_ref[m : m + step_rows, :] = (

time: 46.5 us -> 46.4 us (level)
  no operation moved by 1% of the time
where the time goes in v5:
time: 46.4 us; the launch traced here: 46.1 us
  blocking collectives  30 us (65%)
  starting transfers between devices  6.52 us (14%)
  Pallas kernels  4.79 us (10%)
  waiting for transfers between devices  3.14 us (7%)
  other arithmetic  1.49 us (3%)
    all_to_all x1, blocking collectives, per_device(): received = lax.all_to_all(outgoing, 'azi', 0, 0)  16.9 us
    all_to_all x1, blocking collectives, per_device(): received = lax.all_to_all(solved.reshape(SECTORS, RANK, LANES), 'azi', 0, 0)  13.1 us
    ppermute x1, starting transfers between devices, per_device(): cross = lax.ppermute(cross, ('rad', 'azi'), swaps)  4.03 us
    ppermute x1, waiting for transfers between devices, per_device(): cross = lax.ppermute(cross, ('rad', 'azi'), swaps)  3.14 us
    ppermute x1, starting transfers between devices, per_device(): chip = lax.ppermute(chip, 'azi', [(i, i ^ 1) for i in range(SECTORS)])  2.48 us
    convert_element_type x1, other arithmetic, split_rows(): return (high.astype(BF), (density - high).astype(BF))  1.49 us
    pallas_call x1, Pallas kernels, expand(): call(expand_kernel, [(ROWS, SECTOR, DEPTH)], [VMEM] * 2, [pltpu.VMEM((ROW...  1.46 us
    pallas_call x1, Pallas kernels, solve_edge(): call(edge_kernel, [(SECTORS * RANK, LANES)], [VMEM] * 7, [pltpu.VMEM((LAN...  0.93 us
  transfers between devices with their start and end apart: 2, of which 1 were waited for; matrix products, arithmetic and copies ran while one was open for 0% of the time, Pallas kernels for 2%

profile of v5, /device:TPU:256, one launch (start us, length us, event | category | flops | bytes accessed | tf_op | source)
XLA Modules:
  0.0 46.1 jit_solution(4980095423107996304)
XLA Ops:
  0.0 0.0 copy-start.5
  0.0 1.5 %fusion = (bf16[16,128,128]{2,1,0:T(8,128)(2,1)S(1)}, bf16[16,128,128]{2,1,0:T(8,128)(2,1)S(1)}) fusion(f32[16,128,128]{2,1,0:T(8,128)} %param.7), kind=kLoop, calls=%fused_computation.2 | loop fusion | flops 1048576 | bytes 2097152 | tf_op jit(solution)/shard_map/convert_element_type | solution.py:462
  1.5 0.0 copy-done.5
  1.5 0.0 copy-start.1
  1.5 0.7 %compress.1 = f32[16,72,128]{2,1,0:T(8,128)S(1)} custom-call(bf16[16,128,128]{2,1,0:T(8,128)(2,1)S(1)} %get-tuple-element.18.high_ref, bf16[16,128,128]{2,1,0:T(8,128)(2,1)S(1)} %get-tuple-element.17.low_ref, bf16[96,256]{1,0:T(8,128)(2,1)S(1)} %copy-done.5), custom_call_target="tpu_custom_call" | custom-call | tf_op jit(solution)/shard_map/compress/pallas_call | solution.py:398
  2.2 0.0 copy-start
  2.2 16.9 %all_to_all.10.p_ref = f32[16,72,128]{2,1,0:T(8,128)S(1)} all-to-all(f32[16,72,128]{2,1,0:T(8,128)S(1)} %compress.1), channel_id=1, replica_groups=mesh['rad'=32,'azi'=16] {'azi'}, dimensions={0} | all-to-all | bytes 1179648 | tf_op jit(solution)/shard_map/all_to_all | solution.py:471
  19.2 0.0 copy-done.1
  19.2 0.0 copy-done
  19.2 0.0 copy-start.2
  19.2 0.0 copy-start.3
  19.2 0.8 %make_source.1 = (f32[192,512]{1,0:T(8,128)S(1)}, f32[56,512]{1,0:T(8,128)S(1)}, f32[56,512]{1,0:T(8,128)S(1)}) custom-call(f32[16,72,128]{2,1,0:T(8,128)S(1)} %all_to_all.10.p_ref, bf16[768,512]{1,0:T(8,128)(2,1)S(1)} %copy-done.1, bf16[768,512]{1,0:T(8,128)(2,1)S(1)} %copy-done), custom_call_target="tpu_custom_call" | custom-call | tf_op jit(solution)/shard_map/make_source/pallas_call | solution.py:409
  20.0 4.0 %collective-permute-start = (f32[56,512]{1,0:T(8,128)S(1)}, f32[56,512]{1,0:T(8,128)S(1)}, u32[]{:S(2)}, u32[]{:S(2)}) collective-permute-start(f32[56,512]{1,0:T(8,128)S(1)} %get-tuple-element.15), channel_id=1, source_target_pairs={{1,16},{16,1},{3,18},{18,3},{5,20},{20,5},{7,22},{22,7},{9,24},{24... | collective-permute-start | bytes 344072 | tf_op jit(solution)/shard_map/ppermute | solution.py:476
  24.0 2.5 %collective-permute-start.1 = (f32[56,512]{1,0:T(8,128)S(1)}, f32[56,512]{1,0:T(8,128)S(1)}, u32[]{:S(2)}, u32[]{:S(2)}) collective-permute-start(f32[56,512]{1,0:T(8,128)S(1)} %get-tuple-element.16), channel_id=1, source_target_pairs={{0,1},{1,0},{2,3},{3,2},{4,5},{5,4},{6,7},{7,6},{8,9},{9,8},{10,11... | collective-permute-start | bytes 344072 | tf_op jit(solution)/shard_map/ppermute | solution.py:477
  26.5 0.9 %solve_main.1 = (f32[128,512]{1,0:T(8,128)S(1)}, f32[2,14,8,128]{3,2,1,0:T(8,128)S(1)}, f32[14,2,8,128]{3,2,1,0:T(8,128)S(1)}) custom-call(f32[192,512]{1,0:T(8,128)S(1)} %get-tuple-element.11.s_ref), custom_call_target="tpu_custom_call" | custom-call | flops 40000000 | bytes 1000000 | tf_op jit(solution)/shard_map/solve_main/pallas_call | solution.py:420
  27.4 3.1 %collective-permute-done.cross_ref = f32[56,512]{1,0:T(8,128)S(1)} collective-permute-done((f32[56,512]{1,0:T(8,128)S(1)}, f32[56,512]{1,0:T(8,128)S(1)}, u32[]{:S(2)}, u32[]{:S(2)}) %collective-permute-start) | collective-permute-done | bytes 114720 | tf_op jit(solution)/shard_map/ppermute | solution.py:476
  30.6 0.0 collective-permute-done.1.chip_ref
  30.6 0.0 copy-done.2
  30.6 0.0 copy-done.3
  30.6 0.9 %solve_edge.1 = f32[768,128]{1,0:T(8,128)S(1)} custom-call(f32[128,512]{1,0:T(8,128)S(1)} %get-tuple-element.12.main_ref, f32[2,14,8,128]{3,2,1,0:T(8,128)S(1)} %get-tuple-element.13.inverse_ref, f32[14,2,8,128]{3,2,1,0:T(8,128)S(1)} %get-tuple-element.14.weight_ref, f32[56,512]{1,0:T(8,128)S(1)} %collective-permute-done.cross_ref, ...), custom_call_target="tpu_custom_call" | custom-call | tf_op jit(solution)/shard_map/solve_edge/pallas_call | solution.py:434
  31.5 0.0 copy-start.4
  31.5 13.1 %all_to_all.11.q_ref = f32[16,48,128]{2,1,0:T(8,128)S(1)} all-to-all(f32[16,48,128]{2,1,0:T(8,128)S(1)} %bitcast.1), channel_id=1, replica_groups=mesh['rad'=32,'azi'=16] {'azi'}, dimensions={0} | all-to-all | bytes 786432 | tf_op jit(solution)/shard_map/all_to_all | solution.py:480
  44.6 0.0 copy-done.4
  44.6 1.5 %expand.1 = f32[16,128,128]{2,1,0:T(8,128)} custom-call(f32[16,48,128]{2,1,0:T(8,128)S(1)} %all_to_all.11.q_ref, bf16[128,192]{1,0:T(8,128)(2,1)S(1)} %copy-done.4), custom_call_target="tpu_custom_call" | custom-call | tf_op jit(solution)/shard_map/expand/pallas_call | solution.py:445
Async XLA Ops:
  0.0 1.5 %copy-start.5 = (bf16[96,256]{1,0:T(8,128)(2,1)S(1)}, bf16[96,256]{1,0:T(8,128)(2,1)}, u32[]{:S(2)}) copy-start(bf16[96,256]{1,0:T(8,128)(2,1)} %constant.12.clone.squeeze_ref) | copy-start | bytes 147460
  1.5 17.7 %copy-start.1 = (bf16[768,512]{1,0:T(8,128)(2,1)S(1)}, bf16[768,512]{1,0:T(8,128)(2,1)}, u32[]{:S(2)}) copy-start(bf16[768,512]{1,0:T(8,128)(2,1)} %constant.13.clone.high_ref) | copy-start | bytes 2359300
  2.2 17.0 %copy-start = (bf16[768,512]{1,0:T(8,128)(2,1)S(1)}, bf16[768,512]{1,0:T(8,128)(2,1)}, u32[]{:S(2)}) copy-start(bf16[768,512]{1,0:T(8,128)(2,1)} %constant.14.clone.low_ref) | copy-start | bytes 2359300
  19.2 11.4 %copy-start.2 = (bf16[768,512]{1,0:T(8,128)(2,1)S(1)}, bf16[768,512]{1,0:T(8,128)(2,1)}, u32[]{:S(2)}) copy-start(bf16[768,512]{1,0:T(8,128)(2,1)} %constant.16.clone.vl_ref) | copy-start | bytes 2359300
  19.2 11.4 %copy-start.3 = (bf16[768,512]{1,0:T(8,128)(2,1)S(1)}, bf16[768,512]{1,0:T(8,128)(2,1)}, u32[]{:S(2)}) copy-start(bf16[768,512]{1,0:T(8,128)(2,1)} %constant.15.clone.vh_ref) | copy-start | bytes 2359300
  20.0 10.6 %collective-permute-start = (f32[56,512]{1,0:T(8,128)S(1)}, f32[56,512]{1,0:T(8,128)S(1)}, u32[]{:S(2)}, u32[]{:S(2)}) collective-permute-start(f32[56,512]{1,0:T(8,128)S(1)} %get-tuple-element.15), channel_id=1, source_target_pairs={{1,16},{16,1},{3,18},{18,3},{5,20},{20,5},{7,22},{22,7},{9,24},{24... | collective-permute-start | bytes 344072 | tf_op jit(solution)/shard_map/ppermute | solution.py:476
  24.0 6.6 %collective-permute-start.1 = (f32[56,512]{1,0:T(8,128)S(1)}, f32[56,512]{1,0:T(8,128)S(1)}, u32[]{:S(2)}, u32[]{:S(2)}) collective-permute-start(f32[56,512]{1,0:T(8,128)S(1)} %get-tuple-element.16), channel_id=1, source_target_pairs={{0,1},{1,0},{2,3},{3,2},{4,5},{5,4},{6,7},{7,6},{8,9},{9,8},{10,11... | collective-permute-start | bytes 344072 | tf_op jit(solution)/shard_map/ppermute | solution.py:477
  31.5 13.1 %copy-start.4 = (bf16[128,192]{1,0:T(8,128)(2,1)S(1)}, bf16[128,192]{1,0:T(8,128)(2,1)}, u32[]{:S(2)}) copy-start(bf16[128,192]{1,0:T(8,128)(2,1)} %constant.17.clone.stretch_ref) | copy-start | bytes 147460

commit v6 on v5

--- a/solution.py
+++ b/solution.py
@@ -102,11 +102,10 @@
     return blocks
 
 
-def compress_kernel(high_ref, low_ref, squeeze_ref, out_ref, y_ref):
+def compress_kernel(x_ref, squeeze_ref, out_ref, y_ref):
     squeeze = squeeze_ref[...]
     for r in range(0, ROWS, 2):
-        rows = slice(r, r + 2)
-        pair = [jnp.concatenate([h, l], axis=0) for h, l in zip(high_ref[rows], low_ref[rows])]
+        pair = [jnp.concatenate(halves(x_ref[k]), axis=0) for k in (r, r + 1)]
         y = dot(squeeze, jnp.concatenate(pair, axis=1))
         y = y[:RANK] + y[RANK:]
         y_ref[r] = y[:, :LANES]
@@ -126,37 +125,47 @@
                     out_ref[(g - j) % SECTORS + side, at : at + 8, :] = blocks[g]
 
 
-def source_kernel(p_ref, high_ref, low_ref, s_ref, cross_ref, chip_ref):
-    turned = []
-    for j in range(3):
-        block = p_ref[:, j * HALF : (j + 1) * HALF, :].reshape(SECTORS * HALF, LANES).T
-        turned.append(jnp.concatenate([block[:64], block[64:]], axis=1))
-    cells_high, cells_low = halves(jnp.concatenate(turned, axis=0))
+def pack(ref, at, level):
+    ref[0:8, :] = jnp.where(level < 4, at(2, 3), at(0, 3))
+    ref[8:16, :] = jnp.where(level < 2, pltpu.roll(at(2, 2), 5, 0), at(0, 1))
+    ref[16:24, :] = at(2, 1)
+    ref[24:32, :] = jnp.where(level < 3, at(2, 2), at(0, 2))
+    for d in range(1, 4):
+        ref[24 + 8 * d : 32 + 8 * d, :] = at(1, d)
+
+
+def to_source(ref, cells, high_ref, low_ref):
+    cells_high, cells_low = halves(cells)
+    count = cells.shape[0]
     both = jnp.concatenate([cells_high, cells_low], axis=0)
     for n in range(0, COEFS, 256):
         wide = dot(both, high_ref[:, n : n + 256])
-        s_ref[:, n : n + 256] = (
-            wide[:CELLS] + wide[CELLS:] + dot(cells_high, low_ref[:, n : n + 256])
+        ref[:, n : n + 256] = (
+            wide[:count] + wide[count:] + dot(cells_high, low_ref[:, n : n + 256])
         )
+
+
+def border_kernel(p_ref, high_ref, low_ref, cross_ref, chip_ref, s_ref, inner_ref):
+    outer, inner = [], []
+    for j in range(3):
+        block = p_ref[:, j * HALF : (j + 1) * HALF, :].reshape(SECTORS * HALF, LANES).T
+        block = jnp.concatenate([block[:64], block[64:]], axis=1)
+        outer += [block[:24], block[40:]]
+        inner.append(block[24:40])
+    inner_ref[...] = jnp.concatenate(inner, axis=0)
+    to_source(s_ref, jnp.concatenate(outer, axis=0), high_ref, low_ref)
+    core = lax.axis_index("azi") & 1
     level = lax.broadcasted_iota(jnp.int32, (8, COEFS), 0)
 
-    def at(j, r):
-        return s_ref[pl.ds(pl.multiple_of(j * 64 + r * 8, 8), 8), :]
-
-    def pack(ref, near, middle, far):
-        ref[0:8, :] = jnp.where(level < 4, at(2, far), at(0, far))
-        ref[8:16, :] = jnp.where(level < 2, pltpu.roll(at(2, middle), 5, 0), at(0, near))
-        ref[16:24, :] = at(2, near)
-        ref[24:32, :] = jnp.where(level < 3, at(2, middle), at(0, middle))
-        ref[32:40, :] = at(1, near)
-        ref[40:48, :] = at(1, middle)
-        ref[48:56, :] = at(1, far)
-
-    core = lax.axis_index("azi") & 1
-    start, back = core * 7, 1 - 2 * core
-    pack(cross_ref, start, start + back, start + 2 * back)
-    start, back = 7 - start, -back
-    pack(chip_ref, start, start + back, start + 2 * back)
+    def rows_from(end):
+        def at(j, d):
+            row = end * 3 + d - 1 + end * (4 - 2 * d)
+            return s_ref[pl.ds(pl.multiple_of(j * 48 + row * 8, 8), 8), :]
+
+        return at
+
+    pack(cross_ref, rows_from(core), level)
+    pack(chip_ref, rows_from(1 - core), level)
 
 
 def unpack(load, distance, level):
@@ -196,7 +205,10 @@
     return jnp.where(jnp.full((8, LANES), last), 0.0, 1.0).astype(F32)
 
 
-def main_kernel(count, s_ref, own_ref, inverse_ref, weight_ref):
+def main_kernel(
+    count, s_ref, inner_ref, high_ref, low_ref, own_ref, inverse_ref, weight_ref, middle_ref
+):
+    to_source(middle_ref, inner_ref[...], high_ref, low_ref)
     shape = (8, LANES)
     level = lax.broadcasted_iota(jnp.int32, shape, 0)
     lane = lax.broadcasted_iota(jnp.int32, shape, 1)
@@ -220,13 +232,20 @@
     def _(tile):
         lanes = pl.ds(pl.multiple_of(tile * LANES, LANES), LANES)
         table = tile % 2
+
+        def source(r):
+            if r in (3, 4):
+                starts = [j * 16 + (r - 3) * 8 for j in range(3)]
+                return [middle_ref[start : start + 8, lanes] for start in starts]
+            starts = [j * 48 + (r if r < 3 else r - 2) * 8 for j in range(3)]
+            return [s_ref[start : start + 8, lanes] for start in starts]
+
         given, scale, step = {}, {}, {}
         state = [{} for _ in range(SWEEPS)]
         for newest in range(3, EXTENDED + SWEEPS - 1):
             e = newest
             if e < 11:
-                starts = [j * 64 + (e - 3) * 8 for j in range(3)]
-                given[e] = [s_ref[start : start + 8, lanes] for start in starts]
+                given[e] = source(e - 3)
                 scale[e] = inverse_ref[table, e]
                 step[e] = [g * scale[e] * (1.0 / theta) for g in given[e]]
                 state[0][e] = step[e]
@@ -394,40 +413,40 @@
     )
 
 
-def compress(high, low, squeeze, **options):
+def compress(density, squeeze, **options):
     return call(
         compress_kernel,
         [(SECTORS, 3 * HALF, LANES)],
-        [VMEM] * 3,
+        [VMEM] * 2,
         [pltpu.VMEM((ROWS, RANK, LANES), F32)],
         "compress",
         **options,
-    )(high, low, squeeze)
-
-
-def make_source(received, high, low, **options):
+    )(density, squeeze)
+
+
+def border_source(received, high, low, **options):
     return call(
-        source_kernel,
-        [(CELLS, COEFS), (56, COEFS), (56, COEFS)],
+        border_kernel,
+        [(56, COEFS), (56, COEFS), (144, COEFS), (48, SECTORS * RANK)],
         [VMEM] * 3,
         [],
-        "make_source",
+        "border_source",
         **options,
     )(received, high, low)
 
 
-def solve_main(count, source, **options):
+def solve_main(count, source, inner, high, low, **options):
     return call(
         functools.partial(main_kernel, count),
         [(LANES, COEFS), (2, EXTENDED, 8, LANES), (EXTENDED, 2, 8, LANES)],
-        [VMEM],
-        [],
+        [VMEM] * 4,
+        [pltpu.VMEM((48, COEFS), F32)],
         "solve_main",
         cost_estimate=pl.CostEstimate(
             flops=40_000_000, bytes_accessed=1_000_000, transcendentals=0
         ),
         **options,
-    )(source)
+    )(source, inner, high, low)
 
 
 def solve_edge(main, inverse, weight, cross, chip, v_high, v_low, **options):
@@ -457,25 +476,21 @@
     )(received, stretch)
 
 
-def split_rows(density):
-    high = lax.reduce_precision(density, 8, 7)
-    return high.astype(BF), (density - high).astype(BF)
-
-
 def per_device(density):
     squeeze, forward, inverse, stretch = (
         jax.tree.map(jnp.asarray, item) for item in tables()
     )
     count = lax.axis_size("rad")
-    outgoing = compress(*split_rows(density), squeeze)
+    held = lax.reduce_precision(density, 8, 23)
+    outgoing = compress(held, squeeze)
     received = lax.all_to_all(outgoing, "azi", 0, 0)
-    source, cross, chip = make_source(received, *forward)
+    cross, chip, source, inner = border_source(received, *forward)
     swaps = []
     for device in range(1, (count - 1) * SECTORS, 2):
         swaps += [(device, device + SECTORS - 1), (device + SECTORS - 1, device)]
     cross = lax.ppermute(cross, ("rad", "azi"), swaps)
     chip = lax.ppermute(chip, "azi", [(i, i ^ 1) for i in range(SECTORS)])
-    main, scales, weights = solve_main(count, source)
+    main, scales, weights = solve_main(count, source, inner, *forward)
     solved = solve_edge(main, scales, weights, cross, chip, *inverse)
     received = lax.all_to_all(solved.reshape(SECTORS, RANK, LANES), "azi", 0, 0)
     return expand(received, stretch)

time: 46.4 us -> 46.1 us (level)
    convert_element_type x1 -> x0, other arithmetic: 1.49 us -> none  [split_rows(): return (high.astype(BF), (density - high).astype(BF))]
    reduce_precision x0 -> x1, other arithmetic: none -> 1.3 us  [per_device(): held = lax.reduce_precision(density, 8, 23)]
  transfers between devices with their start and end apart: 2 -> 2, of which waited for: 1 -> 1; matrix products, arithmetic and copies ran while one was open for 0% -> 0% of each run, Pallas kernels for 2% -> 3%
where the time goes in v6:
time: 46.1 us; the launch traced here: 45.8 us
  blocking collectives  30 us (65%)
  starting transfers between devices  6.51 us (14%)
  Pallas kernels  4.97 us (11%)
  waiting for transfers between devices  2.81 us (6%)
  other arithmetic  1.3 us (3%)
    all_to_all x1, blocking collectives, per_device(): received = lax.all_to_all(outgoing, 'azi', 0, 0)  16.9 us
    all_to_all x1, blocking collectives, per_device(): received = lax.all_to_all(solved.reshape(SECTORS, RANK, LANES), 'azi', 0, 0)  13.1 us
    ppermute x1, starting transfers between devices, per_device(): cross = lax.ppermute(cross, ('rad', 'azi'), swaps)  4.01 us
    ppermute x1, waiting for transfers between devices, per_device(): cross = lax.ppermute(cross, ('rad', 'azi'), swaps)  2.81 us
    ppermute x1, starting transfers between devices, per_device(): chip = lax.ppermute(chip, 'azi', [(i, i ^ 1) for i in range(SECTORS)])  2.5 us
    pallas_call x1, Pallas kernels, expand(): call(expand_kernel, [(ROWS, SECTOR, DEPTH)], [VMEM] * 2, [pltpu.VMEM((ROW...  1.46 us
    reduce_precision x1, other arithmetic, per_device(): held = lax.reduce_precision(density, 8, 23)  1.3 us
    pallas_call x1, Pallas kernels, solve_main(): call(functools.partial(main_kernel, count), [(LANES, COEFS), (2, EXTENDED...  1.23 us
  transfers between devices with their start and end apart: 2, of which 1 were waited for; matrix products, arithmetic and copies ran while one was open for 0% of the time, Pallas kernels for 3%

profile of v6, /device:TPU:256, one launch (start us, length us, event | category | flops | bytes accessed | tf_op | source)
XLA Modules:
  0.0 45.8 jit_solution(10286421353502760588)
XLA Ops:
  0.0 0.0 copy-start.5
  0.0 1.3 %reduce_precision.3.x_ref = f32[16,128,128]{2,1,0:T(8,128)S(1)} reduce-precision(f32[16,128,128]{2,1,0:T(8,128)} %param.7), exponent_bits=8, mantissa_bits=23 | non-fusion elementwise | flops 262144 | bytes 2097152 | tf_op jit(solution)/shard_map/reduce_precision | solution.py:484
  1.3 0.0 copy-done.5
  1.3 0.0 copy-start.1
  1.3 0.7 %compress.1 = f32[16,72,128]{2,1,0:T(8,128)S(1)} custom-call(f32[16,128,128]{2,1,0:T(8,128)S(1)} %reduce_precision.3.x_ref, bf16[96,256]{1,0:T(8,128)(2,1)S(1)} %copy-done.5), custom_call_target="tpu_custom_call" | custom-call | tf_op jit(solution)/shard_map/compress/pallas_call | solution.py:417
  2.0 0.0 copy-start
  2.1 16.9 %all_to_all.10.p_ref = f32[16,72,128]{2,1,0:T(8,128)S(1)} all-to-all(f32[16,72,128]{2,1,0:T(8,128)S(1)} %compress.1), channel_id=1, replica_groups=mesh['rad'=32,'azi'=16] {'azi'}, dimensions={0} | all-to-all | bytes 1179648 | tf_op jit(solution)/shard_map/all_to_all | solution.py:486
  19.0 0.0 copy-done.1
  19.0 0.0 copy-done
  19.0 0.6 %border_source.1 = (f32[56,512]{1,0:T(8,128)S(1)}, f32[56,512]{1,0:T(8,128)S(1)}, f32[144,512]{1,0:T(8,128)S(1)}, f32[48,768]{1,0:T(8,128)S(1)}) custom-call(f32[16,72,128]{2,1,0:T(8,128)S(1)} %all_to_all.10.p_ref, bf16[768,512]{1,0:T(8,128)(2,1)S(1)} %copy-done.1, bf16[768,512]{1,0:T(8,128)(2,1)S(1)} %copy-done), custom_call_target="tpu_custom_call" | custom-call | tf_op jit(solution)/shard_map/border_source/pallas_call | solution.py:428
  19.7 4.0 %collective-permute-start = (f32[56,512]{1,0:T(8,128)S(1)}, f32[56,512]{1,0:T(8,128)S(1)}, u32[]{:S(2)}, u32[]{:S(2)}) collective-permute-start(f32[56,512]{1,0:T(8,128)S(1)} %get-tuple-element.17), channel_id=1, source_target_pairs={{1,16},{16,1},{3,18},{18,3},{5,20},{20,5},{7,22},{22,7},{9,24},{24... | collective-permute-start | bytes 344072 | tf_op jit(solution)/shard_map/ppermute | solution.py:491
  23.7 2.5 %collective-permute-start.1 = (f32[56,512]{1,0:T(8,128)S(1)}, f32[56,512]{1,0:T(8,128)S(1)}, u32[]{:S(2)}, u32[]{:S(2)}) collective-permute-start(f32[56,512]{1,0:T(8,128)S(1)} %get-tuple-element.18), channel_id=1, source_target_pairs={{0,1},{1,0},{2,3},{3,2},{4,5},{5,4},{6,7},{7,6},{8,9},{9,8},{10,11... | collective-permute-start | bytes 344072 | tf_op jit(solution)/shard_map/ppermute | solution.py:492
  26.2 0.0 copy-start.2
  26.2 0.0 copy-start.3
  26.2 1.2 %solve_main.1 = (f32[128,512]{1,0:T(8,128)S(1)}, f32[2,14,8,128]{3,2,1,0:T(8,128)S(1)}, f32[14,2,8,128]{3,2,1,0:T(8,128)S(1)}) custom-call(f32[144,512]{1,0:T(8,128)S(1)} %get-tuple-element.12.s_ref, f32[48,768]{1,0:T(8,128)S(1)} %get-tuple-element.13.inner_ref, bf16[768,512]{1,0:T(8,128)(2,1)S(1)} %copy-done.1, bf16[768,512]{1,0:T(8,128)(2,1)S(1)} %copy-done), custom_call_target="tpu_custom_call" | custom-call | flops 40000000 | bytes 1000000 | tf_op jit(solution)/shard_map/solve_main/pallas_call | solution.py:439
  27.4 2.8 %collective-permute-done.cross_ref = f32[56,512]{1,0:T(8,128)S(1)} collective-permute-done((f32[56,512]{1,0:T(8,128)S(1)}, f32[56,512]{1,0:T(8,128)S(1)}, u32[]{:S(2)}, u32[]{:S(2)}) %collective-permute-start) | collective-permute-done | bytes 114720 | tf_op jit(solution)/shard_map/ppermute | solution.py:491
  30.2 0.0 collective-permute-done.1.chip_ref
  30.2 0.0 copy-done.2
  30.3 0.0 copy-done.3
  30.3 0.9 %solve_edge.1 = f32[768,128]{1,0:T(8,128)S(1)} custom-call(f32[128,512]{1,0:T(8,128)S(1)} %get-tuple-element.14.main_ref, f32[2,14,8,128]{3,2,1,0:T(8,128)S(1)} %get-tuple-element.15.inverse_ref, f32[14,2,8,128]{3,2,1,0:T(8,128)S(1)} %get-tuple-element.16.weight_ref, f32[56,512]{1,0:T(8,128)S(1)} %collective-permute-done.cross_ref, ...), custom_call_target="tpu_custom_call" | custom-call | tf_op jit(solution)/shard_map/solve_edge/pallas_call | solution.py:453
  31.2 0.0 copy-start.4
  31.2 13.1 %all_to_all.11.q_ref = f32[16,48,128]{2,1,0:T(8,128)S(1)} all-to-all(f32[16,48,128]{2,1,0:T(8,128)S(1)} %bitcast.1), channel_id=1, replica_groups=mesh['rad'=32,'azi'=16] {'azi'}, dimensions={0} | all-to-all | bytes 786432 | tf_op jit(solution)/shard_map/all_to_all | solution.py:495
  44.3 0.0 copy-done.4
  44.3 1.5 %expand.1 = f32[16,128,128]{2,1,0:T(8,128)} custom-call(f32[16,48,128]{2,1,0:T(8,128)S(1)} %all_to_all.11.q_ref, bf16[128,192]{1,0:T(8,128)(2,1)S(1)} %copy-done.4), custom_call_target="tpu_custom_call" | custom-call | tf_op jit(solution)/shard_map/expand/pallas_call | solution.py:464
Async XLA Ops:
  0.0 1.3 %copy-start.5 = (bf16[96,256]{1,0:T(8,128)(2,1)S(1)}, bf16[96,256]{1,0:T(8,128)(2,1)}, u32[]{:S(2)}) copy-start(bf16[96,256]{1,0:T(8,128)(2,1)} %constant.12.clone.squeeze_ref) | copy-start | bytes 147460
  1.3 17.7 %copy-start.1 = (bf16[768,512]{1,0:T(8,128)(2,1)S(1)}, bf16[768,512]{1,0:T(8,128)(2,1)}, u32[]{:S(2)}) copy-start(bf16[768,512]{1,0:T(8,128)(2,1)} %constant.13.clone.high_ref) | copy-start | bytes 2359300
  2.0 17.0 %copy-start = (bf16[768,512]{1,0:T(8,128)(2,1)S(1)}, bf16[768,512]{1,0:T(8,128)(2,1)}, u32[]{:S(2)}) copy-start(bf16[768,512]{1,0:T(8,128)(2,1)} %constant.14.clone.low_ref) | copy-start | bytes 2359300
  19.7 10.6 %collective-permute-start = (f32[56,512]{1,0:T(8,128)S(1)}, f32[56,512]{1,0:T(8,128)S(1)}, u32[]{:S(2)}, u32[]{:S(2)}) collective-permute-start(f32[56,512]{1,0:T(8,128)S(1)} %get-tuple-element.17), channel_id=1, source_target_pairs={{1,16},{16,1},{3,18},{18,3},{5,20},{20,5},{7,22},{22,7},{9,24},{24... | collective-permute-start | bytes 344072 | tf_op jit(solution)/shard_map/ppermute | solution.py:491
  23.7 6.6 %collective-permute-start.1 = (f32[56,512]{1,0:T(8,128)S(1)}, f32[56,512]{1,0:T(8,128)S(1)}, u32[]{:S(2)}, u32[]{:S(2)}) collective-permute-start(f32[56,512]{1,0:T(8,128)S(1)} %get-tuple-element.18), channel_id=1, source_target_pairs={{0,1},{1,0},{2,3},{3,2},{4,5},{5,4},{6,7},{7,6},{8,9},{9,8},{10,11... | collective-permute-start | bytes 344072 | tf_op jit(solution)/shard_map/ppermute | solution.py:492
  26.2 4.1 %copy-start.2 = (bf16[768,512]{1,0:T(8,128)(2,1)S(1)}, bf16[768,512]{1,0:T(8,128)(2,1)}, u32[]{:S(2)}) copy-start(bf16[768,512]{1,0:T(8,128)(2,1)} %constant.16.clone.vl_ref) | copy-start | bytes 2359300
  26.2 4.1 %copy-start.3 = (bf16[768,512]{1,0:T(8,128)(2,1)S(1)}, bf16[768,512]{1,0:T(8,128)(2,1)}, u32[]{:S(2)}) copy-start(bf16[768,512]{1,0:T(8,128)(2,1)} %constant.15.clone.vh_ref) | copy-start | bytes 2359300
  31.2 13.1 %copy-start.4 = (bf16[128,192]{1,0:T(8,128)(2,1)S(1)}, bf16[128,192]{1,0:T(8,128)(2,1)}, u32[]{:S(2)}) copy-start(bf16[128,192]{1,0:T(8,128)(2,1)} %constant.17.clone.stretch_ref) | copy-start | bytes 147460

commit v7 on v6

--- a/solution.py
+++ b/solution.py
@@ -302,11 +302,8 @@
     return steps, values
 
 
-def edge_kernel(
-    main_ref, inverse_ref, weight_ref, cross_ref, chip_ref, vh_ref, vl_ref, out_ref, own_ref
-):
+def add_reach(main_ref, inverse_ref, weight_ref, edge_ref, side, own_ref):
     level = lax.broadcasted_iota(jnp.int32, (8, LANES), 0)
-    core = lax.axis_index("azi") & 1
     cut = window_cut()
     ratios = factors()
     own_ref[...] = main_ref[...]
@@ -315,7 +312,7 @@
     def _(tile):
         lanes = pl.ds(pl.multiple_of(tile * LANES, LANES), LANES)
         table = tile % 2
-        for ref, turned in ((cross_ref, core), (chip_ref, 1 - core)):
+        for ref, turned in ((edge_ref, side),):
             at = [t + turned * (EXTENDED - 1 - 2 * t) for t in range(6)]
             given = {
                 t: unpack(lambda start: ref[start : start + 8, lanes], 3 - t, level)
@@ -349,6 +346,16 @@
                 own_ref[pl.ds(start, 8), lanes] += jnp.where(level < 4, x[2], x[0])
                 own_ref[pl.ds(start + 8, 8), lanes] += x[1]
 
+
+def chip_kernel(main_ref, inverse_ref, weight_ref, chip_ref, own_ref):
+    core = lax.axis_index("azi") & 1
+    add_reach(main_ref, inverse_ref, weight_ref, chip_ref, 1 - core, own_ref)
+
+
+def edge_kernel(main_ref, inverse_ref, weight_ref, cross_ref, vh_ref, vl_ref, out_ref, own_ref):
+    core = lax.axis_index("azi") & 1
+    add_reach(main_ref, inverse_ref, weight_ref, cross_ref, core, own_ref)
+
     own_high, own_low = halves(own_ref[...])
     both = jnp.concatenate([own_high, own_low], axis=0)
 
@@ -449,15 +456,26 @@
     )(source, inner, high, low)
 
 
-def solve_edge(main, inverse, weight, cross, chip, v_high, v_low, **options):
+def solve_chip(main, inverse, weight, chip, **options):
+    return call(
+        chip_kernel,
+        [(LANES, COEFS)],
+        [VMEM] * 4,
+        [],
+        "solve_chip",
+        **options,
+    )(main, inverse, weight, chip)
+
+
+def solve_edge(main, inverse, weight, cross, v_high, v_low, **options):
     return call(
         edge_kernel,
         [(SECTORS * RANK, LANES)],
-        [VMEM] * 7,
+        [VMEM] * 6,
         [pltpu.VMEM((LANES, COEFS), F32)],
         "solve_edge",
         **options,
-    )(main, inverse, weight, cross, chip, v_high, v_low)
+    )(main, inverse, weight, cross, v_high, v_low)
 
 
 def expand(received, stretch, **options):
@@ -491,7 +509,8 @@
     cross = lax.ppermute(cross, ("rad", "azi"), swaps)
     chip = lax.ppermute(chip, "azi", [(i, i ^ 1) for i in range(SECTORS)])
     main, scales, weights = solve_main(count, source, inner, *forward)
-    solved = solve_edge(main, scales, weights, cross, chip, *inverse)
+    main = solve_chip(main, scales, weights, chip)
+    solved = solve_edge(main, scales, weights, cross, *inverse)
     received = lax.all_to_all(solved.reshape(SECTORS, RANK, LANES), "azi", 0, 0)
     return expand(received, stretch)
 

time: 46.1 us -> 47.9 us (1.039)
  waiting for transfers between devices: 2.81 us -> 4.77 us
    ppermute x1, waiting for transfers between devices: 2.81 us -> 4.76 us  [per_device(): cross = lax.ppermute(cross, ('rad', 'azi'), swaps)]
    ppermute x1, starting transfers between devices: 2.5 us -> 1.97 us  [per_device(): chip = lax.ppermute(chip, 'azi', [(i, i ^ 1) for i in range(SECTORS)])]
where the time goes in v7:
time: 47.9 us; the launch traced here: 47.6 us
  blocking collectives  30.1 us (63%)
  starting transfers between devices  6.37 us (13%)
  Pallas kernels  4.98 us (10%)
  waiting for transfers between devices  4.77 us (10%)
  other arithmetic  1.3 us (3%)
    all_to_all x1, blocking collectives, per_device(): received = lax.all_to_all(outgoing, 'azi', 0, 0)  16.9 us
    all_to_all x1, blocking collectives, per_device(): received = lax.all_to_all(solved.reshape(SECTORS, RANK, LANES), 'azi', 0, 0)  13.1 us
    ppermute x1, waiting for transfers between devices, per_device(): cross = lax.ppermute(cross, ('rad', 'azi'), swaps)  4.76 us
    ppermute x1, starting transfers between devices, per_device(): cross = lax.ppermute(cross, ('rad', 'azi'), swaps)  4.4 us
    ppermute x1, starting transfers between devices, per_device(): chip = lax.ppermute(chip, 'azi', [(i, i ^ 1) for i in range(SECTORS)])  1.97 us
    pallas_call x1, Pallas kernels, expand(): call(expand_kernel, [(ROWS, SECTOR, DEPTH)], [VMEM] * 2, [pltpu.VMEM((ROW...  1.46 us
    reduce_precision x1, other arithmetic, per_device(): held = lax.reduce_precision(density, 8, 23)  1.3 us
    pallas_call x1, Pallas kernels, solve_main(): call(functools.partial(main_kernel, count), [(LANES, COEFS), (2, EXTENDED...  1.22 us
  transfers between devices with their start and end apart: 2, of which 1 were waited for; matrix products, arithmetic and copies ran while one was open for 0% of the time, Pallas kernels for 3%

profile of v7, /device:TPU:256, one launch (start us, length us, event | category | flops | bytes accessed | tf_op | source)
XLA Modules:
  0.0 47.6 jit_solution(8060394705729198569)
XLA Ops:
  0.0 0.0 copy-start.5
  0.0 1.3 %reduce_precision.3.x_ref = f32[16,128,128]{2,1,0:T(8,128)S(1)} reduce-precision(f32[16,128,128]{2,1,0:T(8,128)} %param.7), exponent_bits=8, mantissa_bits=23 | non-fusion elementwise | flops 262144 | bytes 2097152 | tf_op jit(solution)/shard_map/reduce_precision | solution.py:502
  1.3 0.0 copy-done.5
  1.3 0.0 copy-start.1
  1.3 0.7 %compress.1 = f32[16,72,128]{2,1,0:T(8,128)S(1)} custom-call(f32[16,128,128]{2,1,0:T(8,128)S(1)} %reduce_precision.3.x_ref, bf16[96,256]{1,0:T(8,128)(2,1)S(1)} %copy-done.5), custom_call_target="tpu_custom_call" | custom-call | tf_op jit(solution)/shard_map/compress/pallas_call | solution.py:424
  2.0 0.0 copy-start
  2.1 16.9 %all_to_all.10.p_ref = f32[16,72,128]{2,1,0:T(8,128)S(1)} all-to-all(f32[16,72,128]{2,1,0:T(8,128)S(1)} %compress.1), channel_id=1, replica_groups=mesh['rad'=32,'azi'=16] {'azi'}, dimensions={0} | all-to-all | bytes 1179648 | tf_op jit(solution)/shard_map/all_to_all | solution.py:504
  19.0 0.0 copy-done.1
  19.0 0.0 copy-done
  19.0 0.6 %border_source.1 = (f32[56,512]{1,0:T(8,128)S(1)}, f32[56,512]{1,0:T(8,128)S(1)}, f32[144,512]{1,0:T(8,128)S(1)}, f32[48,768]{1,0:T(8,128)S(1)}) custom-call(f32[16,72,128]{2,1,0:T(8,128)S(1)} %all_to_all.10.p_ref, bf16[768,512]{1,0:T(8,128)(2,1)S(1)} %copy-done.1, bf16[768,512]{1,0:T(8,128)(2,1)S(1)} %copy-done), custom_call_target="tpu_custom_call" | custom-call | tf_op jit(solution)/shard_map/border_source/pallas_call | solution.py:435
  19.7 2.0 %collective-permute-start = (f32[56,512]{1,0:T(8,128)S(1)}, f32[56,512]{1,0:T(8,128)S(1)}, u32[]{:S(2)}, u32[]{:S(2)}) collective-permute-start(f32[56,512]{1,0:T(8,128)S(1)} %get-tuple-element.17), channel_id=1, source_target_pairs={{0,1},{1,0},{2,3},{3,2},{4,5},{5,4},{6,7},{7,6},{8,9},{9,8},{10,11... | collective-permute-start | bytes 344072 | tf_op jit(solution)/shard_map/ppermute | solution.py:510
  21.6 4.4 %collective-permute-start.1 = (f32[56,512]{1,0:T(8,128)S(1)}, f32[56,512]{1,0:T(8,128)S(1)}, u32[]{:S(2)}, u32[]{:S(2)}) collective-permute-start(f32[56,512]{1,0:T(8,128)S(1)} %get-tuple-element.18), channel_id=1, source_target_pairs={{1,16},{16,1},{3,18},{18,3},{5,20},{20,5},{7,22},{22,7},{9,24},{24... | collective-permute-start | bytes 344072 | tf_op jit(solution)/shard_map/ppermute | solution.py:509
  26.0 0.0 copy-start.3
  26.0 1.2 %solve_main.1 = (f32[128,512]{1,0:T(8,128)S(1)}, f32[2,14,8,128]{3,2,1,0:T(8,128)S(1)}, f32[14,2,8,128]{3,2,1,0:T(8,128)S(1)}) custom-call(f32[144,512]{1,0:T(8,128)S(1)} %get-tuple-element.12.s_ref, f32[48,768]{1,0:T(8,128)S(1)} %get-tuple-element.13.inner_ref, bf16[768,512]{1,0:T(8,128)(2,1)S(1)} %copy-done.1, bf16[768,512]{1,0:T(8,128)(2,1)S(1)} %copy-done), custom_call_target="tpu_custom_call" | custom-call | flops 40000000 | bytes 1000000 | tf_op jit(solution)/shard_map/solve_main/pallas_call | solution.py:446
  27.3 0.0 copy-start.2
  27.3 0.0 collective-permute-done.chip_ref
  27.3 0.2 solve_chip.1.main_ref
  27.5 4.8 %collective-permute-done.1.cross_ref = f32[56,512]{1,0:T(8,128)S(1)} collective-permute-done((f32[56,512]{1,0:T(8,128)S(1)}, f32[56,512]{1,0:T(8,128)S(1)}, u32[]{:S(2)}, u32[]{:S(2)}) %collective-permute-start.1) | collective-permute-done | bytes 114720 | tf_op jit(solution)/shard_map/ppermute | solution.py:509
  32.3 0.0 copy-done.3
  32.3 0.0 copy-done.2
  32.3 0.8 %solve_edge.1 = f32[768,128]{1,0:T(8,128)S(1)} custom-call(f32[128,512]{1,0:T(8,128)S(1)} %solve_chip.1.main_ref, f32[2,14,8,128]{3,2,1,0:T(8,128)S(1)} %get-tuple-element.15.inverse_ref, f32[14,2,8,128]{3,2,1,0:T(8,128)S(1)} %get-tuple-element.16.weight_ref, f32[56,512]{1,0:T(8,128)S(1)} %collective-permute-done.1.cross_ref, ...), custom_call_target="tpu_custom_call" | custom-call | tf_op jit(solution)/shard_map/solve_edge/pallas_call | solution.py:471
  33.0 0.0 copy-start.4
  33.0 13.1 %all_to_all.11.q_ref = f32[16,48,128]{2,1,0:T(8,128)S(1)} all-to-all(f32[16,48,128]{2,1,0:T(8,128)S(1)} %bitcast.1), channel_id=1, replica_groups=mesh['rad'=32,'azi'=16] {'azi'}, dimensions={0} | all-to-all | bytes 786432 | tf_op jit(solution)/shard_map/all_to_all | solution.py:514
  46.2 0.0 copy-done.4
  46.2 1.5 %expand.1 = f32[16,128,128]{2,1,0:T(8,128)} custom-call(f32[16,48,128]{2,1,0:T(8,128)S(1)} %all_to_all.11.q_ref, bf16[128,192]{1,0:T(8,128)(2,1)S(1)} %copy-done.4), custom_call_target="tpu_custom_call" | custom-call | tf_op jit(solution)/shard_map/expand/pallas_call | solution.py:482
Async XLA Ops:
  0.0 1.3 %copy-start.5 = (bf16[96,256]{1,0:T(8,128)(2,1)S(1)}, bf16[96,256]{1,0:T(8,128)(2,1)}, u32[]{:S(2)}) copy-start(bf16[96,256]{1,0:T(8,128)(2,1)} %constant.12.clone.squeeze_ref) | copy-start | bytes 147460
  1.3 17.7 %copy-start.1 = (bf16[768,512]{1,0:T(8,128)(2,1)S(1)}, bf16[768,512]{1,0:T(8,128)(2,1)}, u32[]{:S(2)}) copy-start(bf16[768,512]{1,0:T(8,128)(2,1)} %constant.13.clone.high_ref) | copy-start | bytes 2359300
  2.0 17.0 %copy-start = (bf16[768,512]{1,0:T(8,128)(2,1)S(1)}, bf16[768,512]{1,0:T(8,128)(2,1)}, u32[]{:S(2)}) copy-start(bf16[768,512]{1,0:T(8,128)(2,1)} %constant.14.clone.low_ref) | copy-start | bytes 2359300
  19.7 7.6 %collective-permute-start = (f32[56,512]{1,0:T(8,128)S(1)}, f32[56,512]{1,0:T(8,128)S(1)}, u32[]{:S(2)}, u32[]{:S(2)}) collective-permute-start(f32[56,512]{1,0:T(8,128)S(1)} %get-tuple-element.17), channel_id=1, source_target_pairs={{0,1},{1,0},{2,3},{3,2},{4,5},{5,4},{6,7},{7,6},{8,9},{9,8},{10,11... | collective-permute-start | bytes 344072 | tf_op jit(solution)/shard_map/ppermute | solution.py:510
  21.6 10.6 %collective-permute-start.1 = (f32[56,512]{1,0:T(8,128)S(1)}, f32[56,512]{1,0:T(8,128)S(1)}, u32[]{:S(2)}, u32[]{:S(2)}) collective-permute-start(f32[56,512]{1,0:T(8,128)S(1)} %get-tuple-element.18), channel_id=1, source_target_pairs={{1,16},{16,1},{3,18},{18,3},{5,20},{20,5},{7,22},{22,7},{9,24},{24... | collective-permute-start | bytes 344072 | tf_op jit(solution)/shard_map/ppermute | solution.py:509
  26.0 6.2 %copy-start.3 = (bf16[768,512]{1,0:T(8,128)(2,1)S(1)}, bf16[768,512]{1,0:T(8,128)(2,1)}, u32[]{:S(2)}) copy-start(bf16[768,512]{1,0:T(8,128)(2,1)} %constant.15.clone.vh_ref) | copy-start | bytes 2359300
  27.3 5.0 %copy-start.2 = (bf16[768,512]{1,0:T(8,128)(2,1)S(1)}, bf16[768,512]{1,0:T(8,128)(2,1)}, u32[]{:S(2)}) copy-start(bf16[768,512]{1,0:T(8,128)(2,1)} %constant.16.clone.vl_ref) | copy-start | bytes 2359300
  33.0 13.1 %copy-start.4 = (bf16[128,192]{1,0:T(8,128)(2,1)S(1)}, bf16[128,192]{1,0:T(8,128)(2,1)}, u32[]{:S(2)}) copy-start(bf16[128,192]{1,0:T(8,128)(2,1)} %constant.17.clone.stretch_ref) | copy-start | bytes 147460

commit v8 on v6

--- a/solution.py
+++ b/solution.py
@@ -69,7 +69,7 @@
         ],
         axis=0,
     )
-    stretch = np.concatenate([left_high, left_high, left_low, left_low], axis=1)
+    stretch = np.concatenate([left_high, left_high, left_low], axis=1)
     return squeeze, forward, inverse, stretch
 
 
@@ -381,7 +381,7 @@
             columns = []
             for k in range(2):
                 high, low = halves(y_ref[r + k])
-                columns.append(jnp.concatenate([high, low, high, low], axis=0))
+                columns.append(jnp.concatenate([high, low, high], axis=0))
             wide = dot(stretch, jnp.concatenate(columns, axis=1))
             out_ref[r] = wide[:, :LANES]
             out_ref[r + 1] = wide[:, LANES:]

time: 46.1 us -> 46 us (level)
  no operation moved by 1% of the time
where the time goes in v8:
time: 46 us; the launch traced here: 45.8 us
  blocking collectives  30 us (65%)
  starting transfers between devices  6.51 us (14%)
  Pallas kernels  4.97 us (11%)
  waiting for transfers between devices  2.81 us (6%)
  other arithmetic  1.3 us (3%)
    all_to_all x1, blocking collectives, per_device(): received = lax.all_to_all(outgoing, 'azi', 0, 0)  16.9 us
    all_to_all x1, blocking collectives, per_device(): received = lax.all_to_all(solved.reshape(SECTORS, RANK, LANES), 'azi', 0, 0)  13.1 us
    ppermute x1, starting transfers between devices, per_device(): cross = lax.ppermute(cross, ('rad', 'azi'), swaps)  4.01 us
    ppermute x1, waiting for transfers between devices, per_device(): cross = lax.ppermute(cross, ('rad', 'azi'), swaps)  2.81 us
    ppermute x1, starting transfers between devices, per_device(): chip = lax.ppermute(chip, 'azi', [(i, i ^ 1) for i in range(SECTORS)])  2.5 us
    pallas_call x1, Pallas kernels, expand(): call(expand_kernel, [(ROWS, SECTOR, DEPTH)], [VMEM] * 2, [pltpu.VMEM((ROW...  1.45 us
    reduce_precision x1, other arithmetic, per_device(): held = lax.reduce_precision(density, 8, 23)  1.3 us
    pallas_call x1, Pallas kernels, solve_main(): call(functools.partial(main_kernel, count), [(LANES, COEFS), (2, EXTENDED...  1.23 us
  transfers between devices with their start and end apart: 2, of which 1 were waited for; matrix products, arithmetic and copies ran while one was open for 0% of the time, Pallas kernels for 3%

profile of v8, /device:TPU:256, one launch (start us, length us, event | category | flops | bytes accessed | tf_op | source)
XLA Modules:
  0.0 45.8 jit_solution(17162788753315224031)
XLA Ops:
  0.0 0.0 copy-start.5
  0.0 1.3 %reduce_precision.3.x_ref = f32[16,128,128]{2,1,0:T(8,128)S(1)} reduce-precision(f32[16,128,128]{2,1,0:T(8,128)} %param.7), exponent_bits=8, mantissa_bits=23 | non-fusion elementwise | flops 262144 | bytes 2097152 | tf_op jit(solution)/shard_map/reduce_precision | solution.py:484
  1.3 0.0 copy-done.5
  1.3 0.0 copy-start.1
  1.3 0.7 %compress.1 = f32[16,72,128]{2,1,0:T(8,128)S(1)} custom-call(f32[16,128,128]{2,1,0:T(8,128)S(1)} %reduce_precision.3.x_ref, bf16[96,256]{1,0:T(8,128)(2,1)S(1)} %copy-done.5), custom_call_target="tpu_custom_call" | custom-call | tf_op jit(solution)/shard_map/compress/pallas_call | solution.py:417
  2.0 0.0 copy-start
  2.1 16.9 %all_to_all.10.p_ref = f32[16,72,128]{2,1,0:T(8,128)S(1)} all-to-all(f32[16,72,128]{2,1,0:T(8,128)S(1)} %compress.1), channel_id=1, replica_groups=mesh['rad'=32,'azi'=16] {'azi'}, dimensions={0} | all-to-all | bytes 1179648 | tf_op jit(solution)/shard_map/all_to_all | solution.py:486
  19.0 0.0 copy-done.1
  19.0 0.0 copy-done
  19.0 0.6 %border_source.1 = (f32[56,512]{1,0:T(8,128)S(1)}, f32[56,512]{1,0:T(8,128)S(1)}, f32[144,512]{1,0:T(8,128)S(1)}, f32[48,768]{1,0:T(8,128)S(1)}) custom-call(f32[16,72,128]{2,1,0:T(8,128)S(1)} %all_to_all.10.p_ref, bf16[768,512]{1,0:T(8,128)(2,1)S(1)} %copy-done.1, bf16[768,512]{1,0:T(8,128)(2,1)S(1)} %copy-done), custom_call_target="tpu_custom_call" | custom-call | tf_op jit(solution)/shard_map/border_source/pallas_call | solution.py:428
  19.7 4.0 %collective-permute-start = (f32[56,512]{1,0:T(8,128)S(1)}, f32[56,512]{1,0:T(8,128)S(1)}, u32[]{:S(2)}, u32[]{:S(2)}) collective-permute-start(f32[56,512]{1,0:T(8,128)S(1)} %get-tuple-element.17), channel_id=1, source_target_pairs={{1,16},{16,1},{3,18},{18,3},{5,20},{20,5},{7,22},{22,7},{9,24},{24... | collective-permute-start | bytes 344072 | tf_op jit(solution)/shard_map/ppermute | solution.py:491
  23.7 2.5 %collective-permute-start.1 = (f32[56,512]{1,0:T(8,128)S(1)}, f32[56,512]{1,0:T(8,128)S(1)}, u32[]{:S(2)}, u32[]{:S(2)}) collective-permute-start(f32[56,512]{1,0:T(8,128)S(1)} %get-tuple-element.18), channel_id=1, source_target_pairs={{0,1},{1,0},{2,3},{3,2},{4,5},{5,4},{6,7},{7,6},{8,9},{9,8},{10,11... | collective-permute-start | bytes 344072 | tf_op jit(solution)/shard_map/ppermute | solution.py:492
  26.2 0.0 copy-start.2
  26.2 0.0 copy-start.3
  26.2 1.2 %solve_main.1 = (f32[128,512]{1,0:T(8,128)S(1)}, f32[2,14,8,128]{3,2,1,0:T(8,128)S(1)}, f32[14,2,8,128]{3,2,1,0:T(8,128)S(1)}) custom-call(f32[144,512]{1,0:T(8,128)S(1)} %get-tuple-element.12.s_ref, f32[48,768]{1,0:T(8,128)S(1)} %get-tuple-element.13.inner_ref, bf16[768,512]{1,0:T(8,128)(2,1)S(1)} %copy-done.1, bf16[768,512]{1,0:T(8,128)(2,1)S(1)} %copy-done), custom_call_target="tpu_custom_call" | custom-call | flops 40000000 | bytes 1000000 | tf_op jit(solution)/shard_map/solve_main/pallas_call | solution.py:439
  27.4 2.8 %collective-permute-done.cross_ref = f32[56,512]{1,0:T(8,128)S(1)} collective-permute-done((f32[56,512]{1,0:T(8,128)S(1)}, f32[56,512]{1,0:T(8,128)S(1)}, u32[]{:S(2)}, u32[]{:S(2)}) %collective-permute-start) | collective-permute-done | bytes 114720 | tf_op jit(solution)/shard_map/ppermute | solution.py:491
  30.2 0.0 collective-permute-done.1.chip_ref
  30.2 0.0 copy-done.2
  30.3 0.0 copy-done.3
  30.3 0.9 %solve_edge.1 = f32[768,128]{1,0:T(8,128)S(1)} custom-call(f32[128,512]{1,0:T(8,128)S(1)} %get-tuple-element.14.main_ref, f32[2,14,8,128]{3,2,1,0:T(8,128)S(1)} %get-tuple-element.15.inverse_ref, f32[14,2,8,128]{3,2,1,0:T(8,128)S(1)} %get-tuple-element.16.weight_ref, f32[56,512]{1,0:T(8,128)S(1)} %collective-permute-done.cross_ref, ...), custom_call_target="tpu_custom_call" | custom-call | tf_op jit(solution)/shard_map/solve_edge/pallas_call | solution.py:453
  31.2 0.0 copy-start.4
  31.2 13.1 %all_to_all.11.q_ref = f32[16,48,128]{2,1,0:T(8,128)S(1)} all-to-all(f32[16,48,128]{2,1,0:T(8,128)S(1)} %bitcast.1), channel_id=1, replica_groups=mesh['rad'=32,'azi'=16] {'azi'}, dimensions={0} | all-to-all | bytes 786432 | tf_op jit(solution)/shard_map/all_to_all | solution.py:495
  44.3 0.0 copy-done.4
  44.3 1.5 %expand.1 = f32[16,128,128]{2,1,0:T(8,128)} custom-call(f32[16,48,128]{2,1,0:T(8,128)S(1)} %all_to_all.11.q_ref, bf16[128,144]{1,0:T(8,128)(2,1)S(1)} %copy-done.4), custom_call_target="tpu_custom_call" | custom-call | tf_op jit(solution)/shard_map/expand/pallas_call | solution.py:464
Async XLA Ops:
  0.0 1.3 %copy-start.5 = (bf16[96,256]{1,0:T(8,128)(2,1)S(1)}, bf16[96,256]{1,0:T(8,128)(2,1)}, u32[]{:S(2)}) copy-start(bf16[96,256]{1,0:T(8,128)(2,1)} %constant.12.clone.squeeze_ref) | copy-start | bytes 147460
  1.3 17.7 %copy-start.1 = (bf16[768,512]{1,0:T(8,128)(2,1)S(1)}, bf16[768,512]{1,0:T(8,128)(2,1)}, u32[]{:S(2)}) copy-start(bf16[768,512]{1,0:T(8,128)(2,1)} %constant.13.clone.high_ref) | copy-start | bytes 2359300
  2.0 17.0 %copy-start = (bf16[768,512]{1,0:T(8,128)(2,1)S(1)}, bf16[768,512]{1,0:T(8,128)(2,1)}, u32[]{:S(2)}) copy-start(bf16[768,512]{1,0:T(8,128)(2,1)} %constant.14.clone.low_ref) | copy-start | bytes 2359300
  19.7 10.6 %collective-permute-start = (f32[56,512]{1,0:T(8,128)S(1)}, f32[56,512]{1,0:T(8,128)S(1)}, u32[]{:S(2)}, u32[]{:S(2)}) collective-permute-start(f32[56,512]{1,0:T(8,128)S(1)} %get-tuple-element.17), channel_id=1, source_target_pairs={{1,16},{16,1},{3,18},{18,3},{5,20},{20,5},{7,22},{22,7},{9,24},{24... | collective-permute-start | bytes 344072 | tf_op jit(solution)/shard_map/ppermute | solution.py:491
  23.7 6.6 %collective-permute-start.1 = (f32[56,512]{1,0:T(8,128)S(1)}, f32[56,512]{1,0:T(8,128)S(1)}, u32[]{:S(2)}, u32[]{:S(2)}) collective-permute-start(f32[56,512]{1,0:T(8,128)S(1)} %get-tuple-element.18), channel_id=1, source_target_pairs={{0,1},{1,0},{2,3},{3,2},{4,5},{5,4},{6,7},{7,6},{8,9},{9,8},{10,11... | collective-permute-start | bytes 344072 | tf_op jit(solution)/shard_map/ppermute | solution.py:492
  26.2 4.1 %copy-start.2 = (bf16[768,512]{1,0:T(8,128)(2,1)S(1)}, bf16[768,512]{1,0:T(8,128)(2,1)}, u32[]{:S(2)}) copy-start(bf16[768,512]{1,0:T(8,128)(2,1)} %constant.16.clone.vl_ref) | copy-start | bytes 2359300
  26.2 4.1 %copy-start.3 = (bf16[768,512]{1,0:T(8,128)(2,1)S(1)}, bf16[768,512]{1,0:T(8,128)(2,1)}, u32[]{:S(2)}) copy-start(bf16[768,512]{1,0:T(8,128)(2,1)} %constant.15.clone.vh_ref) | copy-start | bytes 2359300
  31.2 13.1 %copy-start.4 = (bf16[128,144]{1,0:T(8,128)(2,1)S(1)}, bf16[128,144]{1,0:T(8,128)(2,1)}, u32[]{:S(2)}) copy-start(bf16[128,144]{1,0:T(8,128)(2,1)} %constant.17.clone.stretch_ref) | copy-start | bytes 110596

commit v9 on v6

--- a/solution.py
+++ b/solution.py
@@ -309,7 +309,7 @@
     core = lax.axis_index("azi") & 1
     cut = window_cut()
     ratios = factors()
-    own_ref[...] = main_ref[...]
+    own_ref[48:80, :] = main_ref[48:80, :]
 
     @pl.loop(0, 4, unroll=4)
     def _(tile):
@@ -346,8 +346,9 @@
             for t in range(3, 6):
                 x = state[t]
                 start = pl.multiple_of((at[t] - 3) * 16, 16)
-                own_ref[pl.ds(start, 8), lanes] += jnp.where(level < 4, x[2], x[0])
-                own_ref[pl.ds(start + 8, 8), lanes] += x[1]
+                added = jnp.where(level < 4, x[2], x[0])
+                own_ref[pl.ds(start, 8), lanes] = main_ref[pl.ds(start, 8), lanes] + added
+                own_ref[pl.ds(start + 8, 8), lanes] = main_ref[pl.ds(start + 8, 8), lanes] + x[1]
 
     own_high, own_low = halves(own_ref[...])
     both = jnp.concatenate([own_high, own_low], axis=0)

time: 46.1 us -> 46 us (level)
  no operation moved by 1% of the time
where the time goes in v9:
time: 46 us; the launch traced here: 45.8 us
  blocking collectives  30 us (65%)
  starting transfers between devices  6.51 us (14%)
  Pallas kernels  4.96 us (11%)
  waiting for transfers between devices  2.81 us (6%)
  other arithmetic  1.3 us (3%)
    all_to_all x1, blocking collectives, per_device(): received = lax.all_to_all(outgoing, 'azi', 0, 0)  16.9 us
    all_to_all x1, blocking collectives, per_device(): received = lax.all_to_all(solved.reshape(SECTORS, RANK, LANES), 'azi', 0, 0)  13.1 us
    ppermute x1, starting transfers between devices, per_device(): cross = lax.ppermute(cross, ('rad', 'azi'), swaps)  4.01 us
    ppermute x1, waiting for transfers between devices, per_device(): cross = lax.ppermute(cross, ('rad', 'azi'), swaps)  2.81 us
    ppermute x1, starting transfers between devices, per_device(): chip = lax.ppermute(chip, 'azi', [(i, i ^ 1) for i in range(SECTORS)])  2.5 us
    pallas_call x1, Pallas kernels, expand(): call(expand_kernel, [(ROWS, SECTOR, DEPTH)], [VMEM] * 2, [pltpu.VMEM((ROW...  1.46 us
    reduce_precision x1, other arithmetic, per_device(): held = lax.reduce_precision(density, 8, 23)  1.3 us
    pallas_call x1, Pallas kernels, solve_main(): call(functools.partial(main_kernel, count), [(LANES, COEFS), (2, EXTENDED...  1.23 us
  transfers between devices with their start and end apart: 2, of which 1 were waited for; matrix products, arithmetic and copies ran while one was open for 0% of the time, Pallas kernels for 3%

profile of v9, /device:TPU:256, one launch (start us, length us, event | category | flops | bytes accessed | tf_op | source)
XLA Modules:
  0.0 45.8 jit_solution(2331128362049404902)
XLA Ops:
  0.0 0.0 copy-start.5
  0.0 1.3 %reduce_precision.3.x_ref = f32[16,128,128]{2,1,0:T(8,128)S(1)} reduce-precision(f32[16,128,128]{2,1,0:T(8,128)} %param.7), exponent_bits=8, mantissa_bits=23 | non-fusion elementwise | flops 262144 | bytes 2097152 | tf_op jit(solution)/shard_map/reduce_precision | solution.py:485
  1.3 0.0 copy-done.5
  1.3 0.0 copy-start.1
  1.3 0.7 %compress.1 = f32[16,72,128]{2,1,0:T(8,128)S(1)} custom-call(f32[16,128,128]{2,1,0:T(8,128)S(1)} %reduce_precision.3.x_ref, bf16[96,256]{1,0:T(8,128)(2,1)S(1)} %copy-done.5), custom_call_target="tpu_custom_call" | custom-call | tf_op jit(solution)/shard_map/compress/pallas_call | solution.py:418
  2.0 0.0 copy-start
  2.1 16.9 %all_to_all.10.p_ref = f32[16,72,128]{2,1,0:T(8,128)S(1)} all-to-all(f32[16,72,128]{2,1,0:T(8,128)S(1)} %compress.1), channel_id=1, replica_groups=mesh['rad'=32,'azi'=16] {'azi'}, dimensions={0} | all-to-all | bytes 1179648 | tf_op jit(solution)/shard_map/all_to_all | solution.py:487
  19.0 0.0 copy-done.1
  19.0 0.0 copy-done
  19.0 0.6 %border_source.1 = (f32[56,512]{1,0:T(8,128)S(1)}, f32[56,512]{1,0:T(8,128)S(1)}, f32[144,512]{1,0:T(8,128)S(1)}, f32[48,768]{1,0:T(8,128)S(1)}) custom-call(f32[16,72,128]{2,1,0:T(8,128)S(1)} %all_to_all.10.p_ref, bf16[768,512]{1,0:T(8,128)(2,1)S(1)} %copy-done.1, bf16[768,512]{1,0:T(8,128)(2,1)S(1)} %copy-done), custom_call_target="tpu_custom_call" | custom-call | tf_op jit(solution)/shard_map/border_source/pallas_call | solution.py:429
  19.7 4.0 %collective-permute-start = (f32[56,512]{1,0:T(8,128)S(1)}, f32[56,512]{1,0:T(8,128)S(1)}, u32[]{:S(2)}, u32[]{:S(2)}) collective-permute-start(f32[56,512]{1,0:T(8,128)S(1)} %get-tuple-element.17), channel_id=1, source_target_pairs={{1,16},{16,1},{3,18},{18,3},{5,20},{20,5},{7,22},{22,7},{9,24},{24... | collective-permute-start | bytes 344072 | tf_op jit(solution)/shard_map/ppermute | solution.py:492
  23.7 2.5 %collective-permute-start.1 = (f32[56,512]{1,0:T(8,128)S(1)}, f32[56,512]{1,0:T(8,128)S(1)}, u32[]{:S(2)}, u32[]{:S(2)}) collective-permute-start(f32[56,512]{1,0:T(8,128)S(1)} %get-tuple-element.18), channel_id=1, source_target_pairs={{0,1},{1,0},{2,3},{3,2},{4,5},{5,4},{6,7},{7,6},{8,9},{9,8},{10,11... | collective-permute-start | bytes 344072 | tf_op jit(solution)/shard_map/ppermute | solution.py:493
  26.2 0.0 copy-start.2
  26.2 0.0 copy-start.3
  26.2 1.2 %solve_main.1 = (f32[128,512]{1,0:T(8,128)S(1)}, f32[2,14,8,128]{3,2,1,0:T(8,128)S(1)}, f32[14,2,8,128]{3,2,1,0:T(8,128)S(1)}) custom-call(f32[144,512]{1,0:T(8,128)S(1)} %get-tuple-element.12.s_ref, f32[48,768]{1,0:T(8,128)S(1)} %get-tuple-element.13.inner_ref, bf16[768,512]{1,0:T(8,128)(2,1)S(1)} %copy-done.1, bf16[768,512]{1,0:T(8,128)(2,1)S(1)} %copy-done), custom_call_target="tpu_custom_call" | custom-call | flops 40000000 | bytes 1000000 | tf_op jit(solution)/shard_map/solve_main/pallas_call | solution.py:440
  27.4 2.8 %collective-permute-done.cross_ref = f32[56,512]{1,0:T(8,128)S(1)} collective-permute-done((f32[56,512]{1,0:T(8,128)S(1)}, f32[56,512]{1,0:T(8,128)S(1)}, u32[]{:S(2)}, u32[]{:S(2)}) %collective-permute-start) | collective-permute-done | bytes 114720 | tf_op jit(solution)/shard_map/ppermute | solution.py:492
  30.2 0.0 collective-permute-done.1.chip_ref
  30.2 0.0 copy-done.2
  30.3 0.0 copy-done.3
  30.3 0.9 %solve_edge.1 = f32[768,128]{1,0:T(8,128)S(1)} custom-call(f32[128,512]{1,0:T(8,128)S(1)} %get-tuple-element.14.main_ref, f32[2,14,8,128]{3,2,1,0:T(8,128)S(1)} %get-tuple-element.15.inverse_ref, f32[14,2,8,128]{3,2,1,0:T(8,128)S(1)} %get-tuple-element.16.weight_ref, f32[56,512]{1,0:T(8,128)S(1)} %collective-permute-done.cross_ref, ...), custom_call_target="tpu_custom_call" | custom-call | tf_op jit(solution)/shard_map/solve_edge/pallas_call | solution.py:454
  31.2 0.0 copy-start.4
  31.2 13.1 %all_to_all.11.q_ref = f32[16,48,128]{2,1,0:T(8,128)S(1)} all-to-all(f32[16,48,128]{2,1,0:T(8,128)S(1)} %bitcast.1), channel_id=1, replica_groups=mesh['rad'=32,'azi'=16] {'azi'}, dimensions={0} | all-to-all | bytes 786432 | tf_op jit(solution)/shard_map/all_to_all | solution.py:496
  44.3 0.0 copy-done.4
  44.3 1.5 %expand.1 = f32[16,128,128]{2,1,0:T(8,128)} custom-call(f32[16,48,128]{2,1,0:T(8,128)S(1)} %all_to_all.11.q_ref, bf16[128,192]{1,0:T(8,128)(2,1)S(1)} %copy-done.4), custom_call_target="tpu_custom_call" | custom-call | tf_op jit(solution)/shard_map/expand/pallas_call | solution.py:465
Async XLA Ops:
  0.0 1.3 %copy-start.5 = (bf16[96,256]{1,0:T(8,128)(2,1)S(1)}, bf16[96,256]{1,0:T(8,128)(2,1)}, u32[]{:S(2)}) copy-start(bf16[96,256]{1,0:T(8,128)(2,1)} %constant.12.clone.squeeze_ref) | copy-start | bytes 147460
  1.3 17.7 %copy-start.1 = (bf16[768,512]{1,0:T(8,128)(2,1)S(1)}, bf16[768,512]{1,0:T(8,128)(2,1)}, u32[]{:S(2)}) copy-start(bf16[768,512]{1,0:T(8,128)(2,1)} %constant.13.clone.high_ref) | copy-start | bytes 2359300
  2.0 17.0 %copy-start = (bf16[768,512]{1,0:T(8,128)(2,1)S(1)}, bf16[768,512]{1,0:T(8,128)(2,1)}, u32[]{:S(2)}) copy-start(bf16[768,512]{1,0:T(8,128)(2,1)} %constant.14.clone.low_ref) | copy-start | bytes 2359300
  19.7 10.6 %collective-permute-start = (f32[56,512]{1,0:T(8,128)S(1)}, f32[56,512]{1,0:T(8,128)S(1)}, u32[]{:S(2)}, u32[]{:S(2)}) collective-permute-start(f32[56,512]{1,0:T(8,128)S(1)} %get-tuple-element.17), channel_id=1, source_target_pairs={{1,16},{16,1},{3,18},{18,3},{5,20},{20,5},{7,22},{22,7},{9,24},{24... | collective-permute-start | bytes 344072 | tf_op jit(solution)/shard_map/ppermute | solution.py:492
  23.7 6.6 %collective-permute-start.1 = (f32[56,512]{1,0:T(8,128)S(1)}, f32[56,512]{1,0:T(8,128)S(1)}, u32[]{:S(2)}, u32[]{:S(2)}) collective-permute-start(f32[56,512]{1,0:T(8,128)S(1)} %get-tuple-element.18), channel_id=1, source_target_pairs={{0,1},{1,0},{2,3},{3,2},{4,5},{5,4},{6,7},{7,6},{8,9},{9,8},{10,11... | collective-permute-start | bytes 344072 | tf_op jit(solution)/shard_map/ppermute | solution.py:493
  26.2 4.1 %copy-start.2 = (bf16[768,512]{1,0:T(8,128)(2,1)S(1)}, bf16[768,512]{1,0:T(8,128)(2,1)}, u32[]{:S(2)}) copy-start(bf16[768,512]{1,0:T(8,128)(2,1)} %constant.16.clone.vl_ref) | copy-start | bytes 2359300
  26.2 4.1 %copy-start.3 = (bf16[768,512]{1,0:T(8,128)(2,1)S(1)}, bf16[768,512]{1,0:T(8,128)(2,1)}, u32[]{:S(2)}) copy-start(bf16[768,512]{1,0:T(8,128)(2,1)} %constant.15.clone.vh_ref) | copy-start | bytes 2359300
  31.2 13.1 %copy-start.4 = (bf16[128,192]{1,0:T(8,128)(2,1)S(1)}, bf16[128,192]{1,0:T(8,128)(2,1)}, u32[]{:S(2)}) copy-start(bf16[128,192]{1,0:T(8,128)(2,1)} %constant.17.clone.stretch_ref) | copy-start | bytes 147460
